TPU v7x, 256 devices: a whole 4x4x8 slice. The times are simulated.
256 devices in a mesh: gz: 64 (over z, y, x_lo), gy: 4 (over x_hi, core).
Axes of the slice: x: 4 (x_hi: 2, x_lo: 2; x = x_hi * 2 + x_lo), y: 4, z: 8, core: 2. Of those that a mesh axis runs over, the one named last changes fastest.
Arguments:
- point_feats: bfloat16 [16, 3670016], P(None, ('gz', 'gy')), may hold values from -6 to 6
- cell_index: int32 [3670016], P(('gz', 'gy')), may hold values from 0 to 2047, as said below
- send_slots: int32 [256, 2, 1792], P(('gz', 'gy')), may hold values from 0 to 14335, as said below
- send_count: int32 [256, 2], P(('gz', 'gy')), may hold values from 0 to 1792, as said below
- conv_weight: bfloat16 [16, 4, 3, 3, 3], replicated, may hold values from -0.625 to 0.625
- point_cot: bfloat16 [16, 4587520], P(None, ('gz', 'gy'))
Outputs:
- point_out: bfloat16 [16, 4587520], P(None, ('gz', 'gy'))
- point_grad: bfloat16 [16, 4587520], P(None, ('gz', 'gy'))
- weight_grad: float32 [16, 4, 3, 3, 3], replicated
Inputs may be any that keep to these rules, and one draw needn't show every extreme that they name: `cell_index`: cells are numbered z-plane major, then y, then x within the owner's block; a point on a live list-0 entry lies in its new block's last z-plane, one on a live list-1 entry in its first z-plane. `send_slots`: slots of the device's own points; the live entries of one device are all distinct; entries that are not live are ignored. `send_count`: zero for list 0 of the lowest slab and list 1 of the highest; in every draw some device has 1792 live entries in list 0 and some device in list 1.
All inputs are finite; a program needn't handle non-finite values.
Results may differ from a plain program's by a relative error of at most 0.0056.
Values may be sent and summed in bfloat16 or wider, within the bound.
A program may use at most 64 MiB of HBM per device.

v0:
```python
import math

import jax
import jax.numpy as jnp
from jax import lax
from jax.sharding import PartitionSpec as P

GRP = 4
X = 128
CY = 8
CZ = 2


def padded_2(block, sides, width):
    for axis, dim in sides:
        count = lax.axis_size(axis)
        forward = [(i, i + 1) for i in range(count - 1)]
        backward = [(target, source) for source, target in forward]
        low = lax.ppermute(
            lax.slice_in_dim(block, block.shape[dim] - width, None, axis=dim), axis, forward
        )
        high = lax.ppermute(lax.slice_in_dim(block, 0, width, axis=dim), axis, backward)
        block = jnp.concatenate([low, block, high], axis=dim)
    return block


def shifted(shard, axis, by):
    size = lax.axis_size(axis)
    pairs = [(i, i + by) for i in range(size) if 0 <= i + by < size]
    return lax.ppermute(shard, axis, pairs)


def extend(field):
    padded = padded_2(field, (("gz", 1), ("gy", 2)), 1)
    return jnp.pad(padded, ((0, 0), (0, 0), (0, 0), (1, 1)))


def patches(padded, depth, height, length, flipped):
    pieces = []
    for plane_k in range(3):
        for row_k in range(3):
            for col_k in range(3):
                if flipped:
                    first_z, first_y, first_x = (2 - plane_k, 2 - row_k, 2 - col_k)
                else:
                    first_z, first_y, first_x = (plane_k, row_k, col_k)
                pieces.append(
                    padded[
                        :,
                        first_z : first_z + depth,
                        first_y : first_y + height,
                        first_x : first_x + length,
                    ]
                )
    stacked = jnp.stack(pieces, axis=1)
    return stacked.reshape(stacked.shape[0] // GRP, GRP * 27, depth * height * length)


def block_layout(moved_cells, cell_count):
    slot_total = moved_cells.shape[0]
    block = max(128, min(2048, (1 << 21) // cell_count // 128 * 128))
    block_count = -(-slot_total // block)
    padding = block_count * block - slot_total
    cells_padded = jnp.pad(moved_cells, (0, padding), constant_values=-1).reshape(
        block_count, block
    )
    return (block, block_count, padding, cells_padded)


def one_hot(cells_block, cell_count):
    cell_ids = jnp.arange(cell_count, dtype=jnp.int32)
    return (cells_block[:, None] == cell_ids[None, :]).astype(jnp.bfloat16)


def splat(rows, moved_cells, cell_count):
    block, block_count, padding, cells_padded = block_layout(moved_cells, cell_count)
    row_total = rows.shape[0]
    rows_padded = (
        jnp.pad(rows, ((0, 0), (0, padding)))
        .reshape(row_total, block_count, block)
        .transpose(1, 0, 2)
    )

    def accumulate(carry, inputs):
        rows_block, cells_block = inputs
        table = one_hot(cells_block, cell_count)
        sums = carry[0] + jnp.dot(rows_block, table, preferred_element_type=jnp.float32)
        counts = carry[1] + jnp.sum(table, axis=0, dtype=jnp.float32)
        return ((sums, counts), None)

    start = (jnp.zeros((row_total, cell_count), jnp.float32), jnp.zeros((cell_count,), jnp.float32))
    result, unused = lax.scan(accumulate, start, (rows_padded, cells_padded))
    return result


def read_back(table_vals, moved_cells, cell_count):
    block, block_count, padding, cells_padded = block_layout(moved_cells, cell_count)
    row_total = table_vals.shape[0]

    def select(carry, cells_block):
        table = one_hot(cells_block, cell_count)
        picked = lax.dot_general(
            table_vals, table, (((1,), (1,)), ((), ())), preferred_element_type=jnp.float32
        )
        return (carry, picked.astype(jnp.bfloat16))

    unused, picked_all = lax.scan(select, 0, cells_padded)
    return picked_all.transpose(1, 0, 2).reshape(row_total, block_count * block)[
        :, : moved_cells.shape[0]
    ]


def local(point_feats, cell_index, send_slots, send_count, conv_weight, point_cot):
    channels, own_total = point_feats.shape
    capacity = send_slots.shape[2]
    depth, height, length = (CZ, CY, X)
    cell_count = depth * height * length
    slot_list = send_slots[0]
    count_pair = send_count[0]
    lane_ids = jnp.arange(capacity, dtype=jnp.int32)
    listed = lane_ids[None, :] < count_pair[:, None]
    targets = jnp.where(listed, slot_list, own_total).reshape(-1)
    leaving = jnp.zeros((own_total + 1,), jnp.int32).at[targets].max(1)[:own_total]
    staying = leaving == 0
    zero_feat = jnp.zeros((), point_feats.dtype)
    kept_feats = jnp.where(staying[None], point_feats, zero_feat)
    kept_cells = jnp.where(staying, cell_index, -1)
    flat_slots = slot_list.reshape(-1)
    sent_feats = jnp.take(point_feats, flat_slots, axis=1).reshape(channels, 2, capacity)
    sent_feats = jnp.where(listed[None], sent_feats, zero_feat)
    sent_cells = jnp.where(listed, jnp.take(cell_index, flat_slots).reshape(2, capacity), -1)
    slab = lax.axis_index("gz")
    slab_total = lax.axis_size("gz")
    below_feats, below_cells = shifted((sent_feats[:, 1], sent_cells[1]), "gz", 1)
    above_feats, above_cells = shifted((sent_feats[:, 0], sent_cells[0]), "gz", -1)
    below_cells = jnp.where(slab > 0, below_cells, -1)
    above_cells = jnp.where(slab < slab_total - 1, above_cells, -1)
    moved_feats = jnp.concatenate([kept_feats, below_feats, above_feats], axis=1)
    moved_cells = jnp.concatenate([kept_cells, below_cells, above_cells], axis=0).astype(jnp.int32)
    stacked = jnp.concatenate([moved_feats, point_cot], axis=0)
    sums, counts = splat(stacked, moved_cells, cell_count)
    divisor = jnp.maximum(counts, 1.0)
    grid_vals = (
        (sums[:channels] / divisor).astype(jnp.bfloat16).reshape(channels, depth, height, length)
    )
    cot_sums = sums[channels:]
    groups = channels // GRP
    forward_patches = patches(extend(grid_vals), depth, height, length, False)
    weight_flat = conv_weight.reshape(groups, GRP, GRP * 27)
    preact = jnp.einsum(
        "goj,gjc->goc", weight_flat, forward_patches, preferred_element_type=jnp.float32
    ).reshape(channels, cell_count)
    activ = jax.nn.silu(preact)
    sigma = jax.nn.sigmoid(preact)
    grad_pre = (cot_sums * sigma * (1.0 + preact * (1.0 - sigma))).astype(jnp.bfloat16)
    grad_local = jnp.einsum(
        "goc,gjc->goj",
        grad_pre.reshape(groups, GRP, cell_count),
        forward_patches,
        preferred_element_type=jnp.float32,
    ).reshape(conv_weight.shape)
    cell_all = slab_total * depth * lax.axis_size("gy") * height * length
    weight_grad = lax.psum(grad_local, ("gz", "gy")) / math.sqrt(cell_all)
    back_patches = patches(
        extend(grad_pre.reshape(channels, depth, height, length)), depth, height, length, True
    )
    weight_back = (
        conv_weight.reshape(groups, GRP, GRP, 27)
        .transpose(0, 2, 1, 3)
        .reshape(groups, GRP, GRP * 27)
    )
    grad_grid = jnp.einsum(
        "gij,gjc->gic", weight_back, back_patches, preferred_element_type=jnp.float32
    ).reshape(channels, cell_count)
    cell_table = jnp.concatenate(
        [activ.astype(jnp.bfloat16), (grad_grid / divisor[None]).astype(jnp.bfloat16)], axis=0
    )
    picked = read_back(cell_table, moved_cells, cell_count)
    return (picked[:channels], picked[channels:], weight_grad)


def solution(mesh):
    placed = (
        P(None, ("gz", "gy")),
        P(("gz", "gy")),
        P(("gz", "gy"), None, None),
        P(("gz", "gy"), None),
        P(),
        P(None, ("gz", "gy")),
    )
    return jax.shard_map(
        local,
        mesh=mesh,
        in_specs=placed,
        out_specs=(P(None, ("gz", "gy")), P(None, ("gz", "gy")), P()),
        check_vma=False,
    )
```

profile of v0, /device:TPU:1, one launch (start us, length us, event | category | flops | bytes accessed | tf_op | source)
XLA Modules:
  0.0 326.7 jit_solution(10495415362411631278)
XLA Ops:
  2.3 18.9 %gather_fusion = s32[3584]{0:T(1024)S(1)} fusion(s32[14336]{0:T(1024)S(1)} %copy-done, s32[4096]{0:T(1024)S(1)} %pad_clamp_fusion), kind=kCustom, calls=%fused_computation | custom fusion | bytes 43008 | tf_op jit(solution)/shard_map/jit(_take)/gather | solution.py:131
  21.3 3.2 copy.187
  24.5 8.3 %gather_fusion.1 = bf16[3584,16]{1,0:T(8,128)(2,1)S(1)} fusion(bf16[16,14336]{0,1:T(8,128)(2,1)} %copy.187, s32[4096]{0:T(1024)S(1)} %pad_clamp_fusion), kind=kCustom, calls=%fused_computation.1 | custom fusion | bytes 243712 | tf_op jit(solution)/shard_map/jit(_take)/gather | solution.py:129
  33.2 3.9 %collective-permute-start.2 = (bf16[16,1792]{1,0:T(8,128)(2,1)S(1)}, bf16[16,1792]{1,0:T(8,128)(2,1)S(1)}, u32[]{:S(2)}, u32[]{:S(2)}) collective-permute-start(bf16[16,1792]{1,0:T(8,128)(2,1)S(1)} %get-tuple-element.132), channel_id=1, source_target_pairs={{0,4},{4,8},{8,12},{12,16},{16,20},{20,24},{24,28},{28,32},{32,36}... | collective-permute-start | bytes 172040 | tf_op jit(solution)/shard_map/ppermute | solution.py:30
  38.5 4.0 %collective-permute-start = (s32[1792]{0:T(1024)S(1)}, s32[1792]{0:T(1024)S(1)}, u32[]{:S(2)}, u32[]{:S(2)}) collective-permute-start(s32[1792]{0:T(1024)S(1)} %get-tuple-element.100), channel_id=1, source_target_pairs={{0,4},{4,8},{8,12},{12,16},{16,20},{20,24},{24,28},{28,32},{32,36}... | collective-permute-start | bytes 21512 | tf_op jit(solution)/shard_map/ppermute | solution.py:30
  43.8 25.1 %scatter_custom_fusion = s32[14337]{0:T(1024)S(1)} fusion(s32[3584]{0:T(1024)S(1)} %get-tuple-element.98, s32[3584]{0:T(1024)S(1)} %broadcast.84, s32[]{:T(128)} %copy.330), kind=kCustom, calls=%fused_computation.177 | custom fusion | flops 3584 | bytes 57352 | tf_op jit(solution)/shard_map/scatter-max | solution.py:123
  70.9 51.4 %while.24 = (s32[]{:T(128)}, f32[32,2048]{1,0:T(8,128)S(1)}, f32[2048]{0:T(1024)S(1)}, bf16[18,32,1024]{2,1,0:T(8,128)(2,1)S(1)}, s32[18,1024]{1,0:T(8,128)S(1)}, /*index=5*/s32[]{:T(128)}, s32[]{:T(128)}) while((s32[]{:T(128)}, f32[32,2048]{1,0:T(8,128)S(1)}, f32[2048]{0:T(1024)S(1)}, bf16[18,32,1024]{2,1,0:T(8,128)(2,1)S(1)}, ...), condition=%wide.region_3.4_spmd.clone, body=%wide.region_1.3_spmd.clone.sunk | while | flops 144836608 | bytes 639072 | solution.py:92
  82.3 1.8 fusion.55
  85.2 1.8 fusion.55
  88.0 1.8 fusion.55
  90.9 1.8 fusion.55
  93.8 1.8 fusion.55
  96.6 1.8 fusion.55
  99.5 1.8 fusion.55
  102.3 1.8 fusion.55
  105.2 1.8 fusion.55
  108.0 1.8 fusion.55
  122.4 4.4 %collective-permute-start.4 = (bf16[16,1,8,128]{3,2,1,0:T(8,128)(2,1)S(1)}, bf16[16,1,8,128]{3,2,1,0:T(8,128)(2,1)S(1)}, u32[]{:S(2)}, u32[]{:S(2)}) collective-permute-start(bf16[16,1,8,128]{3,2,1,0:T(8,128)(2,1)S(1)} %get-tuple-element.137), channel_id=1, source_target_pairs={{0,4},{4,8},{8,12},{12,16},{16,20},{20,24},{24,28},{28,32},{32,36}... | collective-permute-start | bytes 98312 | tf_op jit(solution)/shard_map/ppermute | solution.py:19
  128.1 3.3 %collective-permute-done.5 = bf16[16,1,8,128]{3,2,1,0:T(8,128)(2,1)S(1)} collective-permute-done((bf16[16,1,8,128]{3,2,1,0:T(8,128)(2,1)S(1)}, bf16[16,1,8,128]{3,2,1,0:T(8,128)(2,1)S(1)}, u32[]{:S(2)}, u32[]{:S(2)}) %collective-permute-start.5) | collective-permute-done | bytes 32800 | tf_op jit(solution)/shard_map/ppermute | solution.py:22
  131.5 5.5 %collective-permute-start.6 = (bf16[16,4,1,128]{3,2,1,0:T(2,128)(2,1)S(1)}, bf16[16,4,1,128]{3,2,1,0:T(2,128)(2,1)S(1)}, u32[]{:S(2)}, u32[]{:S(2)}) collective-permute-start(bf16[16,4,1,128]{3,2,1,0:T(2,128)(2,1)S(1)} %get-tuple-element.130), channel_id=1, source_target_pairs={{0,1},{1,2},{2,3},{4,5},{5,6},{6,7},{8,9},{9,10},{10,11},{12,13},{... | collective-permute-start | bytes 49160 | tf_op jit(solution)/shard_map/ppermute | solution.py:19
  137.0 1.9 collective-permute-start.7
  139.5 4.2 %collective-permute-done.7 = bf16[16,4,1,128]{3,2,1,0:T(2,128)(2,1)S(1)} collective-permute-done((bf16[16,4,1,128]{3,2,1,0:T(2,128)(2,1)S(1)}, bf16[16,4,1,128]{3,2,1,0:T(2,128)(2,1)S(1)}, u32[]{:S(2)}, u32[]{:S(2)}) %collective-permute-start.7) | collective-permute-done | bytes 16416 | tf_op jit(solution)/shard_map/ppermute | solution.py:22
  162.9 2.0 reshape.165
  166.4 3.8 %collective-permute-start.8 = (bf16[16,1,8,128]{3,2,1,0:T(8,128)(2,1)S(1)}, bf16[16,1,8,128]{3,2,1,0:T(8,128)(2,1)S(1)}, u32[]{:S(2)}, u32[]{:S(2)}) collective-permute-start(bf16[16,1,8,128]{3,2,1,0:T(8,128)(2,1)S(1)} %get-tuple-element.135), channel_id=1, source_target_pairs={{0,4},{4,8},{8,12},{12,16},{16,20},{20,24},{24,28},{28,32},{32,36}... | collective-permute-start | bytes 98312 | tf_op jit(solution)/shard_map/ppermute | solution.py:19
  172.4 88.5 %psum.7 = f32[16,4,3,3,3]{0,4,3,2,1:T(4,128)S(1)} all-reduce(f32[16,4,3,3,3]{0,4,3,2,1:T(4,128)S(1)} %reshape.175), channel_id=1, replica_groups=mesh['gz'=64,'gy'=4] {'gz','gy'}, use_global_device_ids=true, to_apply=%region_6.7 | all-reduce | flops 1728 | bytes 13824 | tf_op jit(solution)/shard_map/psum | solution.py:163
  261.1 3.7 %collective-permute-start.10 = (bf16[16,4,1,128]{3,2,1,0:T(2,128)(2,1)S(1)}, bf16[16,4,1,128]{3,2,1,0:T(2,128)(2,1)S(1)}, u32[]{:S(2)}, u32[]{:S(2)}) collective-permute-start(bf16[16,4,1,128]{3,2,1,0:T(2,128)(2,1)S(1)} %get-tuple-element.128), channel_id=1, source_target_pairs={{0,1},{1,2},{2,3},{4,5},{5,6},{6,7},{8,9},{9,10},{10,11},{12,13},{... | collective-permute-start | bytes 49160 | tf_op jit(solution)/shard_map/ppermute | solution.py:19
  264.7 1.9 collective-permute-start.11
  267.3 4.1 %collective-permute-done.11 = bf16[16,4,1,128]{3,2,1,0:T(2,128)(2,1)S(1)} collective-permute-done((bf16[16,4,1,128]{3,2,1,0:T(2,128)(2,1)S(1)}, bf16[16,4,1,128]{3,2,1,0:T(2,128)(2,1)S(1)}, u32[]{:S(2)}, u32[]{:S(2)}) %collective-permute-start.11) | collective-permute-done | bytes 16416 | tf_op jit(solution)/shard_map/ppermute | solution.py:22
  290.6 2.0 reshape.169
  293.1 32.4 %while.23 = (s32[]{:T(128)}, bf16[18,32,1024]{2,1,0:T(8,128)(2,1)S(1)}, s32[18,1024]{1,0:T(8,128)S(1)}, bf16[32,2048]{1,0:T(8,128)(2,1)S(1)}, s32[]{:T(128)}) while((s32[]{:T(128)}, bf16[18,32,1024]{2,1,0:T(8,128)(2,1)S(1)}, s32[18,1024]{1,0:T(8,128)S(1)}, bf16[32,2048]{1,0:T(8,128)(2,1)S(1)}, s32[]{:T(128)}) %tuple.64), condition=%wide.region_5.6_spmd, body=%wide.region_4.5_spmd.sunk | while | flops 136347648 | bytes 208965 | solution.py:107
  293.1 1.8 fusion.53
  294.9 1.8 fusion.53
  296.7 1.8 fusion.53
  298.5 1.8 fusion.53
  300.3 1.8 fusion.53
  302.1 1.8 fusion.53
  303.9 1.8 fusion.53
  305.7 1.8 fusion.53
  307.5 1.8 fusion.53
  309.3 1.8 fusion.53
  311.1 1.8 fusion.53
  312.9 1.8 fusion.53
  314.7 1.8 fusion.53
  316.5 1.8 fusion.53
  318.3 1.8 fusion.53
  320.1 1.8 fusion.53
  321.9 1.8 fusion.53
  323.7 1.8 fusion.53
  (224 shorter events, 86.2 us)
Async XLA Ops:
  0.6 1.6 copy-start
  2.3 18.9 %copy-start.6 = (s32[1,2,1792]{2,1,0:T(2,128)S(1)}, s32[1,2,1792]{2,1,0:T(2,128)}, u32[]{:S(2)}) copy-start(s32[1,2,1792]{2,1,0:T(2,128)} %param.12) | copy-start | bytes 43012
  2.3 18.9 %copy-start.7 = (s32[1,2]{1,0:T(1,128)S(1)}, s32[1,2]{1,0:T(1,128)}, u32[]{:S(2)}) copy-start(s32[1,2]{1,0:T(1,128)} %param.13) | copy-start | bytes 28
  2.3 19.0 %copy-start.1 = (bf16[16,14336]{1,0:T(8,128)(2,1)S(1)}, bf16[16,14336]{1,0:T(8,128)(2,1)}, u32[]{:S(2)}) copy-start(bf16[16,14336]{1,0:T(8,128)(2,1)} %param.10) | copy-start | bytes 1376260
  32.8 36.3 %copy-start.2 = (bf16[16,17920]{1,0:T(8,128)(2,1)S(1)}, bf16[16,17920]{1,0:T(8,128)(2,1)}, u32[]{:S(2)}) copy-start(bf16[16,17920]{1,0:T(8,128)(2,1)} %param.15) | copy-start | bytes 1720324
  33.2 35.9 %collective-permute-start.2 = (bf16[16,1792]{1,0:T(8,128)(2,1)S(1)}, bf16[16,1792]{1,0:T(8,128)(2,1)S(1)}, u32[]{:S(2)}, u32[]{:S(2)}) collective-permute-start(bf16[16,1792]{1,0:T(8,128)(2,1)S(1)} %get-tuple-element.132), channel_id=1, source_target_pairs={{0,4},{4,8},{8,12},{12,16},{16,20},{20,24},{24,28},{28,32},{32,36}... | collective-permute-start | bytes 172040 | tf_op jit(solution)/shard_map/ppermute | solution.py:30
  37.1 32.0 %collective-permute-start.3 = (bf16[16,1792]{1,0:T(8,128)(2,1)S(1)}, bf16[16,1792]{1,0:T(8,128)(2,1)S(1)}, u32[]{:S(2)}, u32[]{:S(2)}) collective-permute-start(bf16[16,1792]{1,0:T(8,128)(2,1)S(1)} %get-tuple-element.133), channel_id=1, source_target_pairs={{4,0},{8,4},{12,8},{16,12},{20,16},{24,20},{28,24},{32,28},{36,32}... | collective-permute-start | bytes 172040 | tf_op jit(solution)/shard_map/ppermute | solution.py:30
  38.5 30.5 %collective-permute-start = (s32[1792]{0:T(1024)S(1)}, s32[1792]{0:T(1024)S(1)}, u32[]{:S(2)}, u32[]{:S(2)}) collective-permute-start(s32[1792]{0:T(1024)S(1)} %get-tuple-element.100), channel_id=1, source_target_pairs={{0,4},{4,8},{8,12},{12,16},{16,20},{20,24},{24,28},{28,32},{32,36}... | collective-permute-start | bytes 21512 | tf_op jit(solution)/shard_map/ppermute | solution.py:30
  42.5 26.6 %collective-permute-start.1 = (s32[1792]{0:T(1024)S(1)}, s32[1792]{0:T(1024)S(1)}, u32[]{:S(2)}, u32[]{:S(2)}) collective-permute-start(s32[1792]{0:T(1024)S(1)} %get-tuple-element.101), channel_id=1, source_target_pairs={{4,0},{8,4},{12,8},{16,12},{20,16},{24,20},{28,24},{32,28},{36,32}... | collective-permute-start | bytes 21512 | tf_op jit(solution)/shard_map/ppermute | solution.py:30
  70.0 1.0 copy-start.3
  70.9 68.0 %copy-start.5 = (bf16[16,4,3,3,3]{0,1,4,3,2:T(4,128)(2,1)S(1)}, bf16[16,4,3,3,3]{0,1,4,3,2:T(4,128)(2,1)}, u32[]{:S(2)}) copy-start(bf16[16,4,3,3,3]{0,1,4,3,2:T(4,128)(2,1)} %param.14) | copy-start | bytes 10372
  122.3 16.6 %copy-start.4 = (f32[32,2048]{1,0:T(8,128)}, f32[32,2048]{1,0:T(8,128)S(1)}, u32[]{:S(2)}) copy-start(f32[32,2048]{1,0:T(8,128)S(1)} %get-tuple-element.53) | copy-start | bytes 786436
  122.4 5.7 %collective-permute-start.4 = (bf16[16,1,8,128]{3,2,1,0:T(8,128)(2,1)S(1)}, bf16[16,1,8,128]{3,2,1,0:T(8,128)(2,1)S(1)}, u32[]{:S(2)}, u32[]{:S(2)}) collective-permute-start(bf16[16,1,8,128]{3,2,1,0:T(8,128)(2,1)S(1)} %get-tuple-element.137), channel_id=1, source_target_pairs={{0,4},{4,8},{8,12},{12,16},{16,20},{20,24},{24,28},{28,32},{32,36}... | collective-permute-start | bytes 98312 | tf_op jit(solution)/shard_map/ppermute | solution.py:19
  126.7 4.7 %collective-permute-start.5 = (bf16[16,1,8,128]{3,2,1,0:T(8,128)(2,1)S(1)}, bf16[16,1,8,128]{3,2,1,0:T(8,128)(2,1)S(1)}, u32[]{:S(2)}, u32[]{:S(2)}) collective-permute-start(bf16[16,1,8,128]{3,2,1,0:T(8,128)(2,1)S(1)} %get-tuple-element.136), channel_id=1, source_target_pairs={{4,0},{8,4},{12,8},{16,12},{20,16},{24,20},{28,24},{32,28},{36,32}... | collective-permute-start | bytes 98312 | tf_op jit(solution)/shard_map/ppermute | solution.py:22
  131.5 8.0 %collective-permute-start.6 = (bf16[16,4,1,128]{3,2,1,0:T(2,128)(2,1)S(1)}, bf16[16,4,1,128]{3,2,1,0:T(2,128)(2,1)S(1)}, u32[]{:S(2)}, u32[]{:S(2)}) collective-permute-start(bf16[16,4,1,128]{3,2,1,0:T(2,128)(2,1)S(1)} %get-tuple-element.130), channel_id=1, source_target_pairs={{0,1},{1,2},{2,3},{4,5},{5,6},{6,7},{8,9},{9,10},{10,11},{12,13},{... | collective-permute-start | bytes 49160 | tf_op jit(solution)/shard_map/ppermute | solution.py:19
  137.0 6.7 %collective-permute-start.7 = (bf16[16,4,1,128]{3,2,1,0:T(2,128)(2,1)S(1)}, bf16[16,4,1,128]{3,2,1,0:T(2,128)(2,1)S(1)}, u32[]{:S(2)}, u32[]{:S(2)}) collective-permute-start(bf16[16,4,1,128]{3,2,1,0:T(2,128)(2,1)S(1)} %get-tuple-element.131), channel_id=1, source_target_pairs={{1,0},{2,1},{3,2},{5,4},{6,5},{7,6},{9,8},{10,9},{11,10},{13,12},{... | collective-permute-start | bytes 49160 | tf_op jit(solution)/shard_map/ppermute | solution.py:22
  166.4 94.6 %collective-permute-start.8 = (bf16[16,1,8,128]{3,2,1,0:T(8,128)(2,1)S(1)}, bf16[16,1,8,128]{3,2,1,0:T(8,128)(2,1)S(1)}, u32[]{:S(2)}, u32[]{:S(2)}) collective-permute-start(bf16[16,1,8,128]{3,2,1,0:T(8,128)(2,1)S(1)} %get-tuple-element.135), channel_id=1, source_target_pairs={{0,4},{4,8},{8,12},{12,16},{16,20},{20,24},{24,28},{28,32},{32,36}... | collective-permute-start | bytes 98312 | tf_op jit(solution)/shard_map/ppermute | solution.py:19
  171.1 89.9 %collective-permute-start.9 = (bf16[16,1,8,128]{3,2,1,0:T(8,128)(2,1)S(1)}, bf16[16,1,8,128]{3,2,1,0:T(8,128)(2,1)S(1)}, u32[]{:S(2)}, u32[]{:S(2)}) collective-permute-start(bf16[16,1,8,128]{3,2,1,0:T(8,128)(2,1)S(1)} %get-tuple-element.134), channel_id=1, source_target_pairs={{4,0},{8,4},{12,8},{16,12},{20,16},{24,20},{28,24},{32,28},{36,32}... | collective-permute-start | bytes 98312 | tf_op jit(solution)/shard_map/ppermute | solution.py:22
  261.1 6.3 %collective-permute-start.10 = (bf16[16,4,1,128]{3,2,1,0:T(2,128)(2,1)S(1)}, bf16[16,4,1,128]{3,2,1,0:T(2,128)(2,1)S(1)}, u32[]{:S(2)}, u32[]{:S(2)}) collective-permute-start(bf16[16,4,1,128]{3,2,1,0:T(2,128)(2,1)S(1)} %get-tuple-element.128), channel_id=1, source_target_pairs={{0,1},{1,2},{2,3},{4,5},{5,6},{6,7},{8,9},{9,10},{10,11},{12,13},{... | collective-permute-start | bytes 49160 | tf_op jit(solution)/shard_map/ppermute | solution.py:19
  264.7 6.7 %collective-permute-start.11 = (bf16[16,4,1,128]{3,2,1,0:T(2,128)(2,1)S(1)}, bf16[16,4,1,128]{3,2,1,0:T(2,128)(2,1)S(1)}, u32[]{:S(2)}, u32[]{:S(2)}) collective-permute-start(bf16[16,4,1,128]{3,2,1,0:T(2,128)(2,1)S(1)} %get-tuple-element.129), channel_id=1, source_target_pairs={{1,0},{2,1},{3,2},{5,4},{6,5},{7,6},{9,8},{10,9},{11,10},{13,12},{... | collective-permute-start | bytes 49160 | tf_op jit(solution)/shard_map/ppermute | solution.py:22
where the time goes:
time: 328 us; the launch traced here: 327 us
  blocking collectives  88.5 us (27%)
  local copies, waits for them, and re-layouts  67.3 us (21%)
  matrix products  64.8 us (20%)
  other arithmetic  57.8 us (18%)
  starting transfers between devices  34.2 us (10%)
  waiting for transfers between devices  11.7 us (4%)
    psum x1, blocking collectives, local(): weight_grad = lax.psum(grad_local, ('gz', 'gy')) / math.sqrt(cell_all)  88.5 us
    dot_general x18, matrix products, select(): lax.dot_general(table_vals, table, (((1,), (1,)), ((), ())), preferred_el...  32 us
    dot_general x18, matrix products, accumulate(): jnp.dot(rows_block, table, preferred_element_type=jnp.float32)  31.5 us
    unnamed x64, local copies, waits for them, and re-layouts  30.8 us
    another operation x1, other arithmetic, local(): jnp.zeros((own_total + 1,), jnp.int32).at[targets].max(1)[:own_total]  25.1 us
    gather x2, local copies, waits for them, and re-layouts, local(): jnp.take(cell_index, flat_slots).reshape(2, capacity)  18.9 us
    reduce_sum x18, other arithmetic, accumulate(): counts = carry[1] + jnp.sum(table, axis=0, dtype=jnp.float32)  18.6 us
    ppermute x4, starting transfers between devices, padded_2(): lax.ppermute(lax.slice_in_dim(block, block.shape[dim] - width, None, axis...  17.3 us
  transfers between devices with their start and end apart: 12, of which 3 were waited for; matrix products, arithmetic and copies ran while one was open for 8% of the time, Pallas kernels for 0%

commit v1 on v0

v1 whole, which is shorter than its diff:
```python
import functools
import math

import jax
import jax.numpy as jnp
from jax import lax
from jax.experimental import pallas as pl
from jax.experimental.pallas import tpu as pltpu
from jax.sharding import PartitionSpec as P

CH = 16
GRP = 4
X = 128
CY = 8
CZ = 2
S = 1792
OWN = 8
ALL = OWN + 2
LO = 256
MESH = pl.DeviceIdType.MESH
f32 = jnp.float32
bf16 = jnp.bfloat16
NT = (((1,), (1,)), ((), ()))

UP_MSG = tuple(range(4, 12))
DOWN_MSG = (0, 1, 2, 3, 12, 13, 14, 15)
STAY = (0, 1, 2, 3, 8, 9, 10, 11)


def one_hot(row, count):
    ids = lax.broadcasted_iota(jnp.int32, (count, row.shape[1]), 0).astype(f32).astype(bf16)
    return jnp.where(ids == row, jnp.ones((), bf16), jnp.zeros((), bf16))


def masked_rows(row, values, codes):
    zero = jnp.zeros((), bf16)
    return [jnp.where(row == jnp.full((), code, bf16), values, zero) for code in codes]


def sigmoid(v):
    return 1.0 / (1.0 + jnp.exp(-v))


def kernel(
    feats_hbm, cot_hbm, cells_ref, slots_ref, count_ref, weight_ref,
    out_hbm, grad_hbm, wgrad_ref,
    feats, cot, out_buf, grad_buf, onehots, codes, lows, acc, acc_cot,
    list_send, list_recv,
    up_send, down_send, up_recv, down_recv,
    side_send, side_recv, corner_send, corner_recv,
    grid, gpad, patches, gp3, table, divisors, wmat, counts_in, pre,
    part, gather_1, total_1, gather_2,
    load_sem, store_sem, send_sem, recv_sem, send_2, recv_2, red_send, red_recv,
    *, comm,
):
    a = lax.axis_index("gz")
    b = lax.axis_index("gy")
    n_a = lax.axis_size("gz")
    n_b = lax.axis_size("gy")
    z_p = a // 8
    y_p = lax.rem(a // 2, 4)
    x_p = lax.rem(a, 2)

    load_feats = pltpu.make_async_copy(feats_hbm, feats, load_sem.at[0])
    load_cot = pltpu.make_async_copy(cot_hbm, cot, load_sem.at[1])
    load_feats.start()
    load_cot.start()

    def near(da, db):
        return (lax.rem(a + da + n_a, n_a), lax.rem(b + db + n_b, n_b))

    def peer_1(d):
        return (z_p * 8 + lax.rem(y_p + d // 4, 4) * 2 + x_p, lax.rem(b + lax.rem(d, 4), 4))

    def peer_2(d):
        return (lax.rem(z_p + d // 2, 8) * 8 + y_p * 2 + lax.rem(x_p + lax.rem(d, 2), 2), b)

    around = [(da, db) for da in (-1, 0, 1) for db in (-1, 0, 1) if (da, db) != (0, 0)]
    if comm:
        barrier = pltpu.get_barrier_semaphore()
        for da, db in around:
            pl.semaphore_signal(barrier, inc=1, device_id=near(da, db), device_id_type=MESH)

        def greet(d, carry):
            pl.semaphore_signal(barrier, inc=1, device_id=peer_1(d), device_id_type=MESH)
            pl.semaphore_signal(barrier, inc=1, device_id=peer_2(d), device_id_type=MESH)
            return carry

        lax.fori_loop(1, 16, greet, 0)

    tap_row = lax.broadcasted_iota(jnp.int32, (144, 128), 0)
    tap_col = lax.broadcasted_iota(jnp.int32, (144, 128), 1)
    tap_base = jnp.bitwise_and(tap_row, 3) * 27 + jnp.right_shift(tap_row, 4) * 3
    spread = [tap_base + col_k == tap_col for col_k in range(3)]
    out_ch = lax.broadcasted_iota(jnp.int32, (CH, 144), 0)
    in_ch = jnp.bitwise_and(lax.broadcasted_iota(jnp.int32, (CH, 144), 1), 15)
    same_group = jnp.right_shift(out_ch, 2) == jnp.right_shift(in_ch, 2)
    weight = weight_ref[...]
    for col_k in range(3):
        picked = lax.dot_general(
            weight, spread[col_k].astype(bf16), NT, preferred_element_type=f32
        )
        wmat[16 * col_k : 16 * col_k + 16, :] = jnp.where(same_group, picked, 0.0).astype(bf16)

    cells = jnp.concatenate(
        [cells_ref[pl.ds(0, 56, stride=2), :], cells_ref[pl.ds(1, 56, stride=2), :]], axis=1
    )
    cell_y = jnp.right_shift(jnp.bitwise_and(cells, 1023), 7) * 128
    cell_x = jnp.bitwise_and(cells, 127)
    pad = jnp.zeros((8, LO), f32)
    cell_table = jnp.concatenate(
        [cell_y.astype(f32), pad, cell_x.astype(f32), pad], axis=0
    ).astype(bf16)
    lane = lax.broadcasted_iota(jnp.int32, (1, S), 1)
    leaving = jnp.zeros((64, LO), f32)
    for side in range(2):
        listed = lane < count_ref[0, side]
        slot = slots_ref[0, side : side + 1, :]
        slot_hi = jnp.where(listed, jnp.right_shift(slot, 8), -1)
        hot_lo = one_hot(jnp.bitwise_and(slot, 255).astype(f32).astype(bf16), LO)
        hot_hi = lax.broadcasted_iota(jnp.int32, (64, S), 0) == slot_hi
        leaving += lax.dot_general(
            hot_hi.astype(f32).astype(bf16), hot_lo, NT, preferred_element_type=f32
        )
        found = jnp.dot(cell_table, hot_lo, preferred_element_type=f32)
        place = jnp.sum(jnp.where(hot_hi, found[:64] + found[64:], 0.0), axis=0, keepdims=True)
        list_send[side] = jnp.where(listed, place, -1.0)
    code = (
        jnp.bitwise_and(jnp.right_shift(cells, 8), 3) + jnp.right_shift(cells, 10) * 8
    ).astype(f32) + 4.0 * leaving[:56]
    low = jnp.bitwise_and(cells, 255).astype(f32)
    for row in range(7 * OWN):
        k, j = divmod(row, 7)
        codes[k, :, LO * j : LO * (j + 1)] = code[row : row + 1]
        lows[k, :, LO * j : LO * (j + 1)] = low[row : row + 1]

    load_feats.wait()
    acc[...] = jnp.zeros_like(acc)

    def splat_own(k, carry):
        hot = one_hot(lows[k].astype(bf16), LO)
        onehots[k] = hot
        row = codes[k].astype(bf16)
        values = feats[:, pl.ds(pl.multiple_of(k * S, 128), S)]
        rows = masked_rows(row, values, range(16)) + [one_hot(row, 16)]
        acc[...] += lax.dot_general(
            jnp.concatenate(rows, axis=0), hot, NT, preferred_element_type=f32
        )
        return carry

    lax.fori_loop(0, OWN, splat_own, 0)

    counts = acc[256:272, :]
    count_hi = jnp.floor(counts * (1.0 / 256.0))
    count_lo = (counts - 256.0 * count_hi).astype(bf16)
    count_hi = count_hi.astype(bf16)

    def block(number, row):
        lanes = slice(128 * (row % 2), 128 * (row % 2) + 128)
        return acc[16 * number : 16 * number + 16, lanes].astype(bf16)

    def rows_of(numbers, first_row):
        return [block(4 * plane + first_row // 2, first_row) for plane in numbers]

    for ref, members in ((up_send, UP_MSG), (down_send, DOWN_MSG)):
        for i, number in enumerate(members):
            ref[2 * i] = block(number, 0)
            ref[2 * i + 1] = block(number, 1)
        ref[16] = count_lo[:, :128]
        ref[17] = count_lo[:, 128:]
        ref[18] = count_hi[:, :128]
        ref[19] = count_hi[:, 128:]
    for side in range(2):
        lanes = slice(128 * side, 128 * side + 128)
        for i, plane in enumerate(range(4)):
            side_send[side, i] = block(4 * plane + 3 * side, side)
        side_send[side, 4] = count_lo[:, lanes]
        side_send[side, 5] = count_hi[:, lanes]
        for vertical, planes in ((0, (0, 3)), (1, (1, 2))):
            for i, plane in enumerate(planes):
                corner_send[2 * vertical + side, i] = block(4 * plane + 3 * side, side)
            corner_send[2 * vertical + side, 2] = count_lo[:, lanes]
            corner_send[2 * vertical + side, 3] = count_hi[:, lanes]

    copies = []

    def send(src, dst, place, da, db):
        if comm:
            copy = pltpu.make_async_remote_copy(
                src_ref=src, dst_ref=dst, send_sem=send_sem.at[place],
                recv_sem=recv_sem.at[place], device_id=near(da, db), device_id_type=MESH,
            )
            copy.start()
            copies.append(copy)

    if comm:
        pl.semaphore_wait(barrier, len(around) + 30)
    send(list_send.at[0], list_recv.at[1], 0, -1, 0)
    send(list_send.at[1], list_recv.at[0], 1, 1, 0)
    send(up_send, up_recv, 2, 1, 0)
    send(down_send, down_recv, 3, -1, 0)
    for side in range(2):
        db = 2 * side - 1
        send(side_send.at[side], side_recv.at[side], 4 + side, 0, db)
        for vertical in range(2):
            i = 2 * vertical + side
            send(corner_send.at[i], corner_recv.at[i], 6 + i, 2 * vertical - 1, db)

    load_cot.wait()
    acc_cot[...] = jnp.zeros_like(acc_cot)

    def splat_cot(k, carry):
        row = codes[k].astype(bf16)
        values = cot[:, pl.ds(pl.multiple_of(k * S, 128), S)]
        acc_cot[...] += lax.dot_general(
            jnp.concatenate(masked_rows(row, values, STAY), axis=0), onehots[k], NT,
            preferred_element_type=f32,
        )
        return carry

    lax.fori_loop(0, OWN, splat_cot, 0)

    if comm:
        copies[0].wait()
        copies[1].wait()
    for side in range(2):
        present = (a > 0) if side == 0 else (a < n_a - 1)
        place = jnp.where(present, list_recv[side], -1.0).astype(jnp.int32)
        live = place >= 0
        row = jnp.where(live, jnp.right_shift(place, 8) + 8 * side, 16).astype(f32)
        codes[OWN + side] = row
        hot = one_hot(jnp.bitwise_and(place, 255).astype(f32).astype(bf16), LO)
        onehots[OWN + side] = hot
        values = cot[:, (OWN + side) * S : (OWN + side + 1) * S]
        members = STAY[4 * side : 4 * side + 4]
        acc_cot[64 * side : 64 * side + 64, :] += lax.dot_general(
            jnp.concatenate(masked_rows(row.astype(bf16), values, members), axis=0), hot, NT,
            preferred_element_type=f32,
        )

    if comm:
        for copy in copies[2:]:
            copy.wait()
    has_below = a > 0
    has_above = a < n_a - 1
    has_left = b > 0
    has_right = b < n_b - 1

    def unpack(ref, at, flag):
        total = ref[at + 1].astype(f32) * 256.0 + ref[at].astype(f32)
        return jnp.where(flag, total, 0.0)

    for i, (ref, flag) in enumerate(((up_recv, has_below), (down_recv, has_above))):
        for half in range(2):
            total = ref[18 + half].astype(f32) * 256.0 + ref[16 + half].astype(f32)
            counts_in[2 * i + half] = jnp.where(flag, total, 0.0)
    side_flag = (has_right, has_left)
    for side in range(2):
        for i, (ref, at) in enumerate(
            ((side_recv.at[side], 4), (corner_recv.at[side], 2), (corner_recv.at[2 + side], 2))
        ):
            flag = side_flag[side]
            if i == 1:
                flag = jnp.logical_and(flag, has_above)
            if i == 2:
                flag = jnp.logical_and(flag, has_below)
            total = ref[at + 1].astype(f32) * 256.0 + ref[at].astype(f32)
            counts_in[(4 if i == 0 else 4 + 2 * i) + side] = jnp.where(flag, total, 0.0)

    def mean(sums, count):
        return sums / jnp.maximum(count, 1.0)

    sources = (
        (3, up_recv, 4, 2, 0, has_below),
        (0, up_recv, 0, 1, 0, has_below),
        (2, down_recv, 4, 3, 2, has_above),
        (1, down_recv, 0, 0, 2, has_above),
    )
    for plane, (mine, ref, at, theirs, where, flag) in enumerate(sources):
        for row in range(8):
            half = row % 2
            lanes = slice(128 * half, 128 * half + 128)
            number = 4 * mine + row // 2
            other = 4 * theirs + row // 2
            got = ref[2 * (at + row // 2) + half].astype(f32)
            sums = acc[16 * number : 16 * number + 16, lanes] + jnp.where(flag, got, 0.0)
            count = acc[256 + number : 257 + number, lanes]
            count = count + counts_in[where + half, other : other + 1, :]
            divisor = jnp.broadcast_to(jnp.maximum(count, 1.0), (CH, 128))
            grid[plane, 1 + row] = (sums / divisor).astype(bf16)
            if plane in (1, 2):
                divisors[8 * (plane - 1) + row] = divisor
    for side in range(2):
        flag = side_flag[side]
        y_hi = 3 * side
        halo = (
            (3, 1, 1, 2, has_below),
            (0, 1, 0, 1, has_below),
            (2, 0, 1, 3, has_above),
            (1, 0, 0, 0, has_above),
        )
        for plane, (direct, vertical, at, theirs, vertical_flag) in enumerate(halo):
            corner = 2 * vertical + side
            both = jnp.logical_and(flag, vertical_flag)
            sums = jnp.where(flag, side_recv[side, direct].astype(f32), 0.0)
            sums = sums + jnp.where(both, corner_recv[corner, at].astype(f32), 0.0)
            mine = 4 * direct + y_hi
            other = 4 * theirs + y_hi
            kind = 6 if vertical == 0 else 8
            count = counts_in[4 + side, mine : mine + 1, :]
            count = count + counts_in[kind + side, other : other + 1, :]
            grid[plane, 9 * (1 - side)] = mean(sums, count).astype(bf16)

    lane = lax.broadcasted_iota(jnp.int32, (CH, X), 1)
    first_x = lane == 0
    last_x = lane == X - 1
    for z in range(CZ):
        stacked = jnp.concatenate(
            [
                jnp.concatenate([grid[z + u, v + y] for y in range(CY)], axis=1)
                for u in range(3)
                for v in range(3)
            ],
            axis=0,
        )
        patches[z] = stacked
        pre[...] = jnp.dot(wmat[...], stacked, preferred_element_type=f32)
        for y in range(CY):
            lanes = slice(128 * y, 128 * y + 128)
            low_x = pltpu.roll(pre[0:16, lanes], 1, 1)
            high_x = pltpu.roll(pre[32:48, lanes], X - 1, 1)
            value = (
                pre[16:32, lanes]
                + jnp.where(first_x, 0.0, low_x)
                + jnp.where(last_x, 0.0, high_x)
            )
            sigma = sigmoid(value)
            group = 4 * z + y // 2
            half = slice(128 * (y % 2), 128 * (y % 2) + 128)
            table[16 * group : 16 * group + 16, half] = (value * sigma).astype(bf16)
            cot_sum = acc_cot[16 * group : 16 * group + 16, half]
            gpad[z + 1, y + 1] = (cot_sum * sigma * (1.0 + value * (1.0 - sigma))).astype(bf16)

    copies_2 = []

    def send_2nd(src, dst, place, da, db):
        if comm:
            copy = pltpu.make_async_remote_copy(
                src_ref=src, dst_ref=dst, send_sem=send_2.at[place],
                recv_sem=recv_2.at[place], device_id=near(da, db), device_id_type=MESH,
            )
            copy.start()
            copies_2.append(copy)

    send_2nd(gpad.at[1, pl.ds(1, 8)], gpad.at[3, pl.ds(1, 8)], 0, -1, 0)
    send_2nd(gpad.at[2, pl.ds(1, 8)], gpad.at[0, pl.ds(1, 8)], 1, 1, 0)
    send_2nd(gpad.at[pl.ds(1, 2), 1], gpad.at[pl.ds(1, 2), 9], 2, 0, -1)
    send_2nd(gpad.at[pl.ds(1, 2), 8], gpad.at[pl.ds(1, 2), 0], 3, 0, 1)
    send_2nd(gpad.at[1, 1], gpad.at[3, 9], 4, -1, -1)
    send_2nd(gpad.at[1, 8], gpad.at[3, 0], 5, -1, 1)
    send_2nd(gpad.at[2, 1], gpad.at[0, 9], 6, 1, -1)
    send_2nd(gpad.at[2, 8], gpad.at[0, 0], 7, 1, 1)

    def move(plane, row):
        value = gpad[plane, row]
        wide = value.astype(f32)
        gp3[plane, row, 0:16] = jnp.where(last_x, 0.0, pltpu.roll(wide, X - 1, 1)).astype(bf16)
        gp3[plane, row, 16:32] = value
        gp3[plane, row, 32:48] = jnp.where(first_x, 0.0, pltpu.roll(wide, 1, 1)).astype(bf16)

    wide_grad = jnp.zeros((48, 144), f32)
    for z in range(CZ):
        for y in range(CY):
            move(z + 1, y + 1)
        moved = jnp.concatenate([gp3[z + 1, y + 1] for y in range(CY)], axis=1)
        wide_grad += lax.dot_general(moved, patches[z], NT, preferred_element_type=f32)
    compact = jnp.zeros((CH, 128), f32)
    for col_k in range(3):
        kept = jnp.where(same_group, wide_grad[16 * col_k : 16 * col_k + 16], 0.0)
        compact += jnp.dot(
            kept, spread[col_k].astype(f32), preferred_element_type=f32,
            precision=lax.Precision.HIGHEST,
        )
    part[...] = compact

    def spread_1(d):
        return pltpu.make_async_remote_copy(
            src_ref=part, dst_ref=gather_1.at[d - 1], send_sem=red_send.at[0, d - 1],
            recv_sem=red_recv.at[0, d - 1], device_id=peer_1(d), device_id_type=MESH,
        )

    def spread_2(d):
        return pltpu.make_async_remote_copy(
            src_ref=total_1, dst_ref=gather_2.at[d - 1], send_sem=red_send.at[1, d - 1],
            recv_sem=red_recv.at[1, d - 1], device_id=peer_2(d), device_id_type=MESH,
        )

    def start_all(make):
        def body(d, carry):
            make(d).start()
            return carry

        lax.fori_loop(1, 16, body, 0)

    def wait_all(make):
        def body(d, carry):
            make(d).wait()
            return carry

        lax.fori_loop(1, 16, body, 0)

    if comm:
        start_all(spread_1)

    def read_back(into):
        def body(k, carry):
            found = jnp.dot(table[...], onehots[k], preferred_element_type=f32)
            row = codes[k]
            value = jnp.zeros((CH, S), f32)
            for i, number in enumerate(STAY):
                value = jnp.where(row == float(number), found[16 * i : 16 * i + 16], value)
            into[:, pl.ds(pl.multiple_of(k * S, 128), S)] = value.astype(bf16)
            return carry

        lax.fori_loop(0, ALL, body, 0)

    read_back(out_buf)
    store_out = pltpu.make_async_copy(out_buf, out_hbm, store_sem.at[0])
    store_out.start()

    if comm:
        wait_all(spread_1)
    total = part[...]
    for d in range(15):
        total = total + gather_1[d]
    total_1[...] = total
    if comm:
        start_all(spread_2)

    for copy in copies_2:
        copy.wait()
    blank = jnp.zeros((CH, X), bf16)

    def clear(flag, places):
        @pl.when(flag)
        def _():
            for plane, row in places:
                gpad[plane, row] = blank

    clear(a == 0, [(0, row) for row in range(10)])
    clear(a == n_a - 1, [(3, row) for row in range(10)])
    clear(b == 0, [(plane, 0) for plane in range(4)])
    clear(b == n_b - 1, [(plane, 9) for plane in range(4)])
    for plane in range(4):
        for row in range(10):
            if plane in (0, 3) or row in (0, 9):
                move(plane, row)
    result = [None] * 16
    for plane in range(4):
        moved = jnp.concatenate([gp3[plane, row] for row in range(10)], axis=1)
        taps = lax.dot_general(
            wmat[...], moved, (((0,), (0,)), ((), ())), preferred_element_type=f32
        )
        for u in range(3):
            z = plane - 2 + u
            if z not in (0, 1):
                continue
            for v in range(3):
                rows = slice(16 * (3 * u + v), 16 * (3 * u + v) + 16)
                for y in range(CY):
                    source = y + 2 - v
                    term = taps[rows, 128 * source : 128 * source + 128]
                    i = 8 * z + y
                    result[i] = term if result[i] is None else result[i] + term
    for i in range(16):
        group = i // 2
        half = slice(128 * (i % 2), 128 * (i % 2) + 128)
        table[16 * group : 16 * group + 16, half] = (result[i] / divisors[i]).astype(bf16)
    read_back(grad_buf)
    store_grad = pltpu.make_async_copy(grad_buf, grad_hbm, store_sem.at[1])
    store_grad.start()

    if comm:
        wait_all(spread_2)
    total = total_1[...]
    for d in range(15):
        total = total + gather_2[d]
    wgrad_ref[...] = total * (1.0 / math.sqrt(CZ * CY * X * n_a * n_b))
    store_out.wait()
    store_grad.wait()


def fused(feats, cot, cells, slots, count, weight, comm=True):
    hbm = pl.BlockSpec(memory_space=pl.ANY)
    vmem = pl.BlockSpec(memory_space=pltpu.VMEM)
    smem = pl.BlockSpec(memory_space=pltpu.SMEM)
    slots_all = ALL * S
    dma = pltpu.SemaphoreType.DMA
    return pl.pallas_call(
        functools.partial(kernel, comm=comm),
        out_shape=[
            jax.ShapeDtypeStruct((CH, slots_all), bf16),
            jax.ShapeDtypeStruct((CH, slots_all), bf16),
            jax.ShapeDtypeStruct((CH, 128), f32),
        ],
        in_specs=[hbm, hbm, vmem, vmem, smem, vmem],
        out_specs=[hbm, hbm, vmem],
        scratch_shapes=[
            pltpu.VMEM((CH, OWN * S), bf16),
            pltpu.VMEM((CH, slots_all), bf16),
            pltpu.VMEM((CH, slots_all), bf16),
            pltpu.VMEM((CH, slots_all), bf16),
            pltpu.VMEM((ALL, LO, S), bf16),
            pltpu.VMEM((ALL, 1, S), f32),
            pltpu.VMEM((OWN, 1, S), f32),
            pltpu.VMEM((272, LO), f32),
            pltpu.VMEM((128, LO), f32),
            pltpu.VMEM((2, 1, S), f32),
            pltpu.VMEM((2, 1, S), f32),
            pltpu.VMEM((20, CH, 128), bf16),
            pltpu.VMEM((20, CH, 128), bf16),
            pltpu.VMEM((20, CH, 128), bf16),
            pltpu.VMEM((20, CH, 128), bf16),
            pltpu.VMEM((2, 6, CH, 128), bf16),
            pltpu.VMEM((2, 6, CH, 128), bf16),
            pltpu.VMEM((4, 4, CH, 128), bf16),
            pltpu.VMEM((4, 4, CH, 128), bf16),
            pltpu.VMEM((4, 10, CH, 128), bf16),
            pltpu.VMEM((4, 10, CH, 128), bf16),
            pltpu.VMEM((CZ, 144, CY * X), bf16),
            pltpu.VMEM((4, 10, 48, 128), bf16),
            pltpu.VMEM((128, LO), bf16),
            pltpu.VMEM((16, CH, 128), f32),
            pltpu.VMEM((48, 144), bf16),
            pltpu.VMEM((10, CH, 128), f32),
            pltpu.VMEM((48, CY * X), f32),
            pltpu.VMEM((CH, 128), f32),
            pltpu.VMEM((15, CH, 128), f32),
            pltpu.VMEM((CH, 128), f32),
            pltpu.VMEM((15, CH, 128), f32),
            dma((2,)),
            dma((2,)),
            dma((10,)),
            dma((10,)),
            dma((8,)),
            dma((8,)),
            dma((2, 15)),
            dma((2, 15)),
        ],
        compiler_params=pltpu.CompilerParams(
            vmem_limit_bytes=48 << 20,
            **(dict(collective_id=0, has_side_effects=True) if comm else {}),
        ),
    )(feats, cot, cells, slots, count, weight)


def local(point_feats, cell_index, send_slots, send_count, conv_weight, point_cot):
    cells = cell_index.reshape(-1, 128)
    weight = jnp.pad(conv_weight.reshape(CH, GRP * 27), ((0, 0), (0, 128 - GRP * 27)))
    out, grad, wgrad = fused(point_feats, point_cot, cells, send_slots, send_count, weight)
    return out, grad, wgrad[:, : GRP * 27].reshape(conv_weight.shape)


def solution(mesh):
    placed = (
        P(None, ("gz", "gy")),
        P(("gz", "gy")),
        P(("gz", "gy"), None, None),
        P(("gz", "gy"), None),
        P(),
        P(None, ("gz", "gy")),
    )
    return jax.shard_map(
        local,
        mesh=mesh,
        in_specs=placed,
        out_specs=(P(None, ("gz", "gy")), P(None, ("gz", "gy")), P()),
        check_vma=False,
    )
```

time: 328 us -> 43.3 us (0.13)
  blocking collectives: 88.5 us -> 0 us
  matrix products: 64.8 us -> 0 us
  local copies, waits for them, and re-layouts: 67.3 us -> 6.03 us
  other arithmetic: 57.8 us -> 0 us
  Pallas kernels: 0 us -> 36.3 us
  starting transfers between devices: 34.2 us -> 0 us
  waiting for transfers between devices: 11.7 us -> 0 us
    psum x1 -> x0, blocking collectives: 88.5 us -> none  [local(): weight_grad = lax.psum(grad_local, ('gz', 'gy')) / math.sqrt(cell_all)]
    dot_general x39 -> x0, matrix products: 64.8 us -> none  [the longest x18 32 us: select(): lax.dot_general(table_vals, table, (((1,), (1,)), ((), ())), preferred_el...]
    pallas_call x0 -> x1, Pallas kernels: none -> 36.3 us  [fused(): pl.pallas_call(functools.partial(kernel, comm=comm), out_shape=[jax.Shape...]
    ppermute x12 -> x0, starting transfers between devices: 34.2 us -> none  [the longest x4 17.3 us: padded_2(): lax.ppermute(lax.slice_in_dim(block, block.shape[dim] - width, None, axis...]
    gather x4 -> x0, local copies, waits for them, and re-layouts: 27.5 us -> none  [the longest x2 18.9 us: local(): jnp.take(cell_index, flat_slots).reshape(2, capacity)]
    another operation x1 -> x0, other arithmetic: 25.1 us -> none  [local(): jnp.zeros((own_total + 1,), jnp.int32).at[targets].max(1)[:own_total]]
    unnamed x64 -> x14, local copies, waits for them, and re-layouts: 30.8 us -> 5.78 us
    reduce_sum x18 -> x0, other arithmetic: 18.6 us -> none  [accumulate(): counts = carry[1] + jnp.sum(table, axis=0, dtype=jnp.float32)]
  transfers between devices with their start and end apart: 12 -> 0, of which waited for: 3 -> 0; matrix products, arithmetic and copies ran while one was open for 8% -> 0% of each run, Pallas kernels for 0% -> 0%
where the time goes in v1:
time: 43.3 us; the launch traced here: 43 us
  Pallas kernels  36.3 us (84%)
  local copies, waits for them, and re-layouts  6.03 us (14%)
  between operations  0.68 us (2%)
    pallas_call x1, Pallas kernels, fused(): pl.pallas_call(functools.partial(kernel, comm=comm), out_shape=[jax.Shape...  36.3 us
    unnamed x14, local copies, waits for them, and re-layouts  5.78 us

profile of v1, /device:TPU:1, one launch (start us, length us, event | category | flops | bytes accessed | tf_op | source)
XLA Modules:
  0.0 43.0 jit_solution(9123113458133665947)
XLA Ops:
  0.6 0.8 %copy.11 = bf16[16,4,3,3,3]{0,4,3,2,1:T(4,128)(2,1)S(1)} copy(bf16[16,4,3,3,3]{0,1,4,3,2:T(4,128)(2,1)} %param.10) | data formatting | bytes 6912 | tf_op args[4]
  1.4 0.0 copy-start.2
  1.4 0.0 copy-start.3
  1.5 0.1 copy.12
  1.5 0.0 copy-start.4
  1.5 0.7 %copy-done.2 = s32[14336]{0:T(1024)S(1)} copy-done((s32[14336]{0:T(1024)S(1)}, s32[14336]{0:T(1024)}, u32[]{:S(2)}) %copy-start.2) | copy-done | bytes 57368
  2.2 0.0 copy-done.3
  2.2 0.0 copy-done.4
  2.2 0.0 copy-start
  2.2 1.1 %copy-done = bf16[16,17920]{1,0:T(8,128)(2,1)S(1)} copy-done((bf16[16,17920]{1,0:T(8,128)(2,1)S(1)}, bf16[16,17920]{1,0:T(8,128)(2,1)}, u32[]{:S(2)}) %copy-start) | copy-done | bytes 573464
  3.3 0.0 copy-start.1
  3.3 1.0 %copy-done.1 = bf16[16,14336]{1,0:T(8,128)(2,1)S(1)} copy-done((bf16[16,14336]{1,0:T(8,128)(2,1)S(1)}, bf16[16,14336]{1,0:T(8,128)(2,1)}, u32[]{:S(2)}) %copy-start.1) | copy-done | bytes 458776
  4.3 36.3 %shard_map.85 = (bf16[16,17920]{1,0:T(8,128)(2,1)S(1)}, bf16[16,17920]{1,0:T(8,128)(2,1)S(1)}, f32[16,128]{1,0:T(8,128)S(1)}) custom-call(bf16[16,14336]{1,0:T(8,128)(2,1)S(1)} %copy-done.1, bf16[16,17920]{1,0:T(8,128)(2,1)S(1)} %copy-done, s32[112,128]{1,0:T(8,128)S(1)} %bitcast.6, s32[1,2,1792]{2,1,0:T(2,128)S(1)} %copy-done.3, s32[1,2]{1,0:T(1,128)S(1)} %copy-done.4, ...), custom_call_target="tpu_custom_call" | custom-call | tf_op jit(solution)/shard_map/pallas_call | solution.py:499
  40.6 0.1 copy.13
  40.7 0.6 %copy.14 = f32[16,4,3,3,3]{0,1,4,3,2:T(4,128)} copy(f32[16,4,3,3,3]{0,4,3,2,1:T(4,128)S(1)} %reshape.17) | data formatting | bytes 13824
  41.4 0.8 %copy.17 = bf16[16,17920]{1,0:T(8,128)(2,1)} copy(bf16[16,17920]{1,0:T(8,128)(2,1)S(1)} %get-tuple-element.18) | data formatting | bytes 1146880
  42.2 0.8 %copy.18 = bf16[16,17920]{1,0:T(8,128)(2,1)} copy(bf16[16,17920]{1,0:T(8,128)(2,1)S(1)} %get-tuple-element.19) | data formatting | bytes 1146880
  (3 shorter events, 0.1 us)
Async XLA Ops:
  1.4 0.8 %copy-start.2 = (s32[14336]{0:T(1024)S(1)}, s32[14336]{0:T(1024)}, u32[]{:S(2)}) copy-start(s32[14336]{0:T(1024)} %param.7) | copy-start | bytes 172036
  1.4 0.8 %copy-start.3 = (s32[1,2,1792]{2,1,0:T(2,128)S(1)}, s32[1,2,1792]{2,1,0:T(2,128)}, u32[]{:S(2)}) copy-start(s32[1,2,1792]{2,1,0:T(2,128)} %slots_ref.1) | copy-start | bytes 43012
  1.5 0.7 %copy-start.4 = (s32[1,2]{1,0:T(1,128)S(1)}, s32[1,2]{1,0:T(1,128)}, u32[]{:S(2)}) copy-start(s32[1,2]{1,0:T(1,128)} %count_ref.1) | copy-start | bytes 28
  2.2 1.1 %copy-start = (bf16[16,17920]{1,0:T(8,128)(2,1)S(1)}, bf16[16,17920]{1,0:T(8,128)(2,1)}, u32[]{:S(2)}) copy-start(bf16[16,17920]{1,0:T(8,128)(2,1)} %cot_hbm.1) | copy-start | bytes 1720324
  3.3 1.0 %copy-start.1 = (bf16[16,14336]{1,0:T(8,128)(2,1)S(1)}, bf16[16,14336]{1,0:T(8,128)(2,1)}, u32[]{:S(2)}) copy-start(bf16[16,14336]{1,0:T(8,128)(2,1)} %feats_hbm.1) | copy-start | bytes 1376260

commit v2 on v1

--- a/solution.py
+++ b/solution.py
@@ -90,12 +90,14 @@
 
     tap_row = lax.broadcasted_iota(jnp.int32, (144, 128), 0)
     tap_col = lax.broadcasted_iota(jnp.int32, (144, 128), 1)
-    tap_base = jnp.bitwise_and(tap_row, 3) * 27 + jnp.right_shift(tap_row, 4) * 3
-    spread = [tap_base + col_k == tap_col for col_k in range(3)]
+    tap_base = jnp.bitwise_and(tap_row, 3) + jnp.right_shift(tap_row, 4) * (3 * GRP)
+    spread = [tap_base + GRP * col_k == tap_col for col_k in range(3)]
     out_ch = lax.broadcasted_iota(jnp.int32, (CH, 144), 0)
     in_ch = jnp.bitwise_and(lax.broadcasted_iota(jnp.int32, (CH, 144), 1), 15)
     same_group = jnp.right_shift(out_ch, 2) == jnp.right_shift(in_ch, 2)
-    weight = weight_ref[...]
+    weight = jnp.concatenate(
+        [weight_ref[i].astype(f32) for i in range(27)] + [jnp.zeros((20, CH), f32)], axis=0
+    ).T.astype(bf16)
     for col_k in range(3):
         picked = lax.dot_general(
             weight, spread[col_k].astype(bf16), NT, preferred_element_type=f32
@@ -148,7 +150,7 @@
         )
         return carry
 
-    lax.fori_loop(0, OWN, splat_own, 0)
+    lax.fori_loop(0, OWN, splat_own, 0, unroll=4)
 
     counts = acc[256:272, :]
     count_hi = jnp.floor(counts * (1.0 / 256.0))
@@ -218,7 +220,7 @@
         )
         return carry
 
-    lax.fori_loop(0, OWN, splat_cot, 0)
+    lax.fori_loop(0, OWN, splat_cot, 0, unroll=4)
 
     if comm:
         copies[0].wait()
@@ -422,7 +424,7 @@
             into[:, pl.ds(pl.multiple_of(k * S, 128), S)] = value.astype(bf16)
             return carry
 
-        lax.fori_loop(0, ALL, body, 0)
+        lax.fori_loop(0, ALL, body, 0, unroll=5)
 
     read_back(out_buf)
     store_out = pltpu.make_async_copy(out_buf, out_hbm, store_sem.at[0])
@@ -485,7 +487,9 @@
     total = total_1[...]
     for d in range(15):
         total = total + gather_2[d]
-    wgrad_ref[...] = total * (1.0 / math.sqrt(CZ * CY * X * n_a * n_b))
+    total = (total * (1.0 / math.sqrt(CZ * CY * X * n_a * n_b))).T
+    for i in range(27):
+        wgrad_ref[i] = total[GRP * i : GRP * i + GRP]
     store_out.wait()
     store_grad.wait()
 
@@ -501,7 +505,7 @@
         out_shape=[
             jax.ShapeDtypeStruct((CH, slots_all), bf16),
             jax.ShapeDtypeStruct((CH, slots_all), bf16),
-            jax.ShapeDtypeStruct((CH, 128), f32),
+            jax.ShapeDtypeStruct((27, GRP, CH), f32),
         ],
         in_specs=[hbm, hbm, vmem, vmem, smem, vmem],
         out_specs=[hbm, hbm, vmem],
@@ -548,7 +552,7 @@
             dma((2, 15)),
         ],
         compiler_params=pltpu.CompilerParams(
-            vmem_limit_bytes=48 << 20,
+            vmem_limit_bytes=60 << 20,
             **(dict(collective_id=0, has_side_effects=True) if comm else {}),
         ),
     )(feats, cot, cells, slots, count, weight)
@@ -556,9 +560,9 @@
 
 def local(point_feats, cell_index, send_slots, send_count, conv_weight, point_cot):
     cells = cell_index.reshape(-1, 128)
-    weight = jnp.pad(conv_weight.reshape(CH, GRP * 27), ((0, 0), (0, 128 - GRP * 27)))
+    weight = conv_weight.transpose(2, 3, 4, 1, 0).reshape(27, GRP, CH)
     out, grad, wgrad = fused(point_feats, point_cot, cells, send_slots, send_count, weight)
-    return out, grad, wgrad[:, : GRP * 27].reshape(conv_weight.shape)
+    return out, grad, wgrad.reshape(3, 3, 3, GRP, CH).transpose(4, 3, 0, 1, 2)
 
 
 def solution(mesh):

time: 43.3 us -> 40.2 us (0.928)
  local copies, waits for them, and re-layouts: 6.03 us -> 3.43 us
    unnamed x14 -> x7, local copies, waits for them, and re-layouts: 5.78 us -> 3.43 us
where the time goes in v2:
time: 40.2 us; the launch traced here: 40 us
  Pallas kernels  35.9 us (89%)
  local copies, waits for them, and re-layouts  3.43 us (9%)
  between operations  0.65 us (2%)
    pallas_call x1, Pallas kernels, fused(): pl.pallas_call(functools.partial(kernel, comm=comm), out_shape=[jax.Shape...  35.9 us
    unnamed x7, local copies, waits for them, and re-layouts  3.43 us

profile of v2, /device:TPU:1, one launch (start us, length us, event | category | flops | bytes accessed | tf_op | source)
XLA Modules:
  0.0 40.0 jit_solution(9509460970078204056)
XLA Ops:
  0.6 35.9 %shard_map.85 = (bf16[16,17920]{1,0:T(8,128)(2,1)}, bf16[16,17920]{1,0:T(8,128)(2,1)}, f32[27,4,16]{2,1,0:T(4,128)}) custom-call(bf16[16,14336]{1,0:T(8,128)(2,1)} %feats_hbm.1, bf16[16,17920]{1,0:T(8,128)(2,1)} %cot_hbm.1, s32[112,128]{1,0:T(8,128)} %bitcast.7, s32[1,2,1792]{2,1,0:T(2,128)} %slots_ref.1, s32[1,2]{1,0:T(1,128)} %count_ref.1, ...), custom_call_target="tpu_custom_call" | custom-call | tf_op jit(solution)/shard_map/pallas_call | solution.py:503
  36.5 0.0 copy-start
  36.5 2.0 %copy.12 = bf16[16,17920]{1,0:T(8,128)(2,1)} copy(bf16[16,17920]{1,0:T(8,128)(2,1)} %get-tuple-element.12) | data formatting | bytes 1146880
  38.5 0.0 copy-done
  38.5 0.0 copy-start.1
  38.5 0.8 %copy.13 = bf16[16,17920]{1,0:T(8,128)(2,1)} copy(bf16[16,17920]{1,0:T(8,128)(2,1)S(1)} %copy-done) | data formatting | bytes 1146880
  39.3 0.0 copy-done.1
  39.3 0.6 %copy.14 = f32[16,4,3,3,3]{0,1,4,3,2:T(4,128)} copy(f32[16,4,3,3,3]{0,1,4,3,2:T(4,128)S(1)} %bitcast.8) | data formatting | bytes 13824
Async XLA Ops:
  36.5 2.0 %copy-start = (bf16[16,17920]{1,0:T(8,128)(2,1)S(1)}, bf16[16,17920]{1,0:T(8,128)(2,1)}, u32[]{:S(2)}) copy-start(bf16[16,17920]{1,0:T(8,128)(2,1)} %get-tuple-element.13) | copy-start | bytes 1720324
  38.5 0.8 %copy-start.1 = (f32[27,4,16]{2,1,0:T(4,128)S(1)}, f32[27,4,16]{2,1,0:T(4,128)}, u32[]{:S(2)}) copy-start(f32[27,4,16]{2,1,0:T(4,128)} %get-tuple-element.8) | copy-start | bytes 20740

commit v3 on v2

--- a/solution.py
+++ b/solution.py
@@ -41,16 +41,23 @@
     return 1.0 / (1.0 + jnp.exp(-v))
 
 
+def select(found, row):
+    value = jnp.zeros((CH, S), f32)
+    for i, number in enumerate(STAY):
+        value = jnp.where(row == float(number), found[16 * i : 16 * i + 16], value)
+    return value.astype(bf16)
+
+
 def kernel(
-    feats_hbm, cot_hbm, cells_ref, slots_ref, count_ref, weight_ref,
-    out_hbm, grad_hbm, wgrad_ref,
-    feats, cot, out_buf, grad_buf, onehots, codes, lows, acc, acc_cot,
+    feats_hbm, cot_hbm, cells_hbm, slots_hbm, count_hbm, weight_hbm,
+    onehots, codes, table, out_buf, wgrad_ref,
+    feats, cot, cells_ref, slots_ref, count_ref, weight_ref, lows, acc, acc_cot,
     list_send, list_recv,
     up_send, down_send, up_recv, down_recv,
     side_send, side_recv, corner_send, corner_recv,
-    grid, gpad, patches, gp3, table, divisors, wmat, counts_in, pre,
-    part, gather_1, total_1, gather_2,
-    load_sem, store_sem, send_sem, recv_sem, send_2, recv_2, red_send, red_recv,
+    grid, gpad, patches, gp3, act, divisors, wmat, counts_in, pre,
+    part, gather_1, row_sum, gather_2, full,
+    load_sem, send_sem, recv_sem, send_2, recv_2, red_send, red_recv,
     *, comm,
 ):
     a = lax.axis_index("gz")
@@ -61,32 +68,38 @@
     y_p = lax.rem(a // 2, 4)
     x_p = lax.rem(a, 2)
 
-    load_feats = pltpu.make_async_copy(feats_hbm, feats, load_sem.at[0])
-    load_cot = pltpu.make_async_copy(cot_hbm, cot, load_sem.at[1])
-    load_feats.start()
-    load_cot.start()
+    loads = [
+        pltpu.make_async_copy(src, dst, load_sem.at[i])
+        for i, (src, dst) in enumerate(
+            (
+                (cells_hbm, cells_ref), (slots_hbm, slots_ref), (count_hbm, count_ref),
+                (feats_hbm, feats), (weight_hbm, weight_ref), (cot_hbm, cot),
+            )
+        )
+    ]
+    for load in loads:
+        load.start()
+    load_cells, load_slots, load_count, load_feats, load_weight, load_cot = loads
+
+    a_near = {-1: lax.rem(a + n_a - 1, n_a), 0: a, 1: lax.rem(a + 1, n_a)}
+    b_all = [b] + [lax.rem(b + k, n_b) for k in range(1, 4)]
+    z_all = [z_p] + [lax.rem(z_p + k, 8) for k in range(1, 8)]
+    y_all = [y_p] + [lax.rem(y_p + k, 4) for k in range(1, 4)]
+    peers_1 = [(z_p * 8 + x_p + y_all[d // 4] * 2, b_all[d % 4]) for d in range(1, 16)]
+    rows_1 = [y_all[d // 4] * 4 + b_all[d % 4] for d in range(1, 16)]
+    peers_2 = [
+        (z_all[d // 2] * 8 + y_p * 2 + (1 - x_p if d % 2 else x_p), b) for d in range(1, 16)
+    ]
+    my_row = y_p * 4 + b
 
     def near(da, db):
-        return (lax.rem(a + da + n_a, n_a), lax.rem(b + db + n_b, n_b))
-
-    def peer_1(d):
-        return (z_p * 8 + lax.rem(y_p + d // 4, 4) * 2 + x_p, lax.rem(b + lax.rem(d, 4), 4))
-
-    def peer_2(d):
-        return (lax.rem(z_p + d // 2, 8) * 8 + y_p * 2 + lax.rem(x_p + lax.rem(d, 2), 2), b)
+        return (a_near[da], b_all[db % 4])
 
     around = [(da, db) for da in (-1, 0, 1) for db in (-1, 0, 1) if (da, db) != (0, 0)]
     if comm:
         barrier = pltpu.get_barrier_semaphore()
-        for da, db in around:
-            pl.semaphore_signal(barrier, inc=1, device_id=near(da, db), device_id_type=MESH)
-
-        def greet(d, carry):
-            pl.semaphore_signal(barrier, inc=1, device_id=peer_1(d), device_id_type=MESH)
-            pl.semaphore_signal(barrier, inc=1, device_id=peer_2(d), device_id_type=MESH)
-            return carry
-
-        lax.fori_loop(1, 16, greet, 0)
+        for place in [near(da, db) for da, db in around] + peers_1 + peers_2:
+            pl.semaphore_signal(barrier, inc=1, device_id=place, device_id_type=MESH)
 
     tap_row = lax.broadcasted_iota(jnp.int32, (144, 128), 0)
     tap_col = lax.broadcasted_iota(jnp.int32, (144, 128), 1)
@@ -95,15 +108,9 @@
     out_ch = lax.broadcasted_iota(jnp.int32, (CH, 144), 0)
     in_ch = jnp.bitwise_and(lax.broadcasted_iota(jnp.int32, (CH, 144), 1), 15)
     same_group = jnp.right_shift(out_ch, 2) == jnp.right_shift(in_ch, 2)
-    weight = jnp.concatenate(
-        [weight_ref[i].astype(f32) for i in range(27)] + [jnp.zeros((20, CH), f32)], axis=0
-    ).T.astype(bf16)
-    for col_k in range(3):
-        picked = lax.dot_general(
-            weight, spread[col_k].astype(bf16), NT, preferred_element_type=f32
-        )
-        wmat[16 * col_k : 16 * col_k + 16, :] = jnp.where(same_group, picked, 0.0).astype(bf16)
-
+    load_cells.wait()
+    load_slots.wait()
+    load_count.wait()
     cells = jnp.concatenate(
         [cells_ref[pl.ds(0, 56, stride=2), :], cells_ref[pl.ds(1, 56, stride=2), :]], axis=1
     )
@@ -116,7 +123,7 @@
     lane = lax.broadcasted_iota(jnp.int32, (1, S), 1)
     leaving = jnp.zeros((64, LO), f32)
     for side in range(2):
-        listed = lane < count_ref[0, side]
+        listed = lane < count_ref[:, side : side + 1]
         slot = slots_ref[0, side : side + 1, :]
         slot_hi = jnp.where(listed, jnp.right_shift(slot, 8), -1)
         hot_lo = one_hot(jnp.bitwise_and(slot, 255).astype(f32).astype(bf16), LO)
@@ -207,6 +214,16 @@
         for vertical in range(2):
             i = 2 * vertical + side
             send(corner_send.at[i], corner_recv.at[i], 6 + i, 2 * vertical - 1, db)
+
+    load_weight.wait()
+    weight = jnp.concatenate(
+        [weight_ref[i].astype(f32) for i in range(27)] + [jnp.zeros((20, CH), f32)], axis=0
+    ).T.astype(bf16)
+    for col_k in range(3):
+        picked = lax.dot_general(
+            weight, spread[col_k].astype(bf16), NT, preferred_element_type=f32
+        )
+        wmat[16 * col_k : 16 * col_k + 16, :] = jnp.where(same_group, picked, 0.0).astype(bf16)
 
     load_cot.wait()
     acc_cot[...] = jnp.zeros_like(acc_cot)
@@ -339,7 +356,7 @@
             sigma = sigmoid(value)
             group = 4 * z + y // 2
             half = slice(128 * (y % 2), 128 * (y % 2) + 128)
-            table[16 * group : 16 * group + 16, half] = (value * sigma).astype(bf16)
+            act[16 * group : 16 * group + 16, half] = (value * sigma).astype(bf16)
             cot_sum = acc_cot[16 * group : 16 * group + 16, half]
             gpad[z + 1, y + 1] = (cot_sum * sigma * (1.0 + value * (1.0 - sigma))).astype(bf16)
 
@@ -379,68 +396,58 @@
     compact = jnp.zeros((CH, 128), f32)
     for col_k in range(3):
         kept = jnp.where(same_group, wide_grad[16 * col_k : 16 * col_k + 16], 0.0)
-        compact += jnp.dot(
-            kept, spread[col_k].astype(f32), preferred_element_type=f32,
-            precision=lax.Precision.HIGHEST,
-        )
-    part[...] = compact
-
-    def spread_1(d):
-        return pltpu.make_async_remote_copy(
-            src_ref=part, dst_ref=gather_1.at[d - 1], send_sem=red_send.at[0, d - 1],
-            recv_sem=red_recv.at[0, d - 1], device_id=peer_1(d), device_id_type=MESH,
-        )
-
-    def spread_2(d):
-        return pltpu.make_async_remote_copy(
-            src_ref=total_1, dst_ref=gather_2.at[d - 1], send_sem=red_send.at[1, d - 1],
-            recv_sem=red_recv.at[1, d - 1], device_id=peer_2(d), device_id_type=MESH,
-        )
-
-    def start_all(make):
-        def body(d, carry):
-            make(d).start()
+        first = kept.astype(bf16)
+        rest = kept - first.astype(f32)
+        second = rest.astype(bf16)
+        third = (rest - second.astype(f32)).astype(bf16)
+        picked = jnp.dot(
+            jnp.concatenate([first, second, third], axis=0), spread[col_k].astype(bf16),
+            preferred_element_type=f32,
+        )
+        compact += picked[0:16] + picked[16:32] + picked[32:48]
+    for i in range(CH):
+        part[i] = compact[i : i + 1]
+
+    def reduce_send(step, peers, sources, targets):
+        if comm:
+            for place, src, dst in zip(peers, sources, targets):
+                pltpu.make_async_remote_copy(
+                    src_ref=src, dst_ref=dst, send_sem=red_send.at[step],
+                    recv_sem=red_recv.at[step], device_id=place, device_id_type=MESH,
+                ).start()
+
+    def reduce_wait(step, buffer):
+        if comm:
+            pltpu.make_async_copy(buffer, buffer, red_send.at[step]).wait()
+            pltpu.make_async_copy(buffer, buffer, red_recv.at[step]).wait()
+
+    reduce_send(0, peers_1, [part.at[r] for r in rows_1], [gather_1.at[d] for d in range(15)])
+
+    def read_back(group):
+        def body(k, carry):
+            found = jnp.dot(act[...], onehots[k], preferred_element_type=f32)
+            out_buf[:, pl.ds(pl.multiple_of(k * S, 128), S)] = select(found, codes[k])
             return carry
 
-        lax.fori_loop(1, 16, body, 0)
-
-    def wait_all(make):
-        def body(d, carry):
-            make(d).wait()
-            return carry
-
-        lax.fori_loop(1, 16, body, 0)
-
-    if comm:
-        start_all(spread_1)
-
-    def read_back(into):
-        def body(k, carry):
-            found = jnp.dot(table[...], onehots[k], preferred_element_type=f32)
-            row = codes[k]
-            value = jnp.zeros((CH, S), f32)
-            for i, number in enumerate(STAY):
-                value = jnp.where(row == float(number), found[16 * i : 16 * i + 16], value)
-            into[:, pl.ds(pl.multiple_of(k * S, 128), S)] = value.astype(bf16)
-            return carry
-
-        lax.fori_loop(0, ALL, body, 0, unroll=5)
-
-    read_back(out_buf)
-    store_out = pltpu.make_async_copy(out_buf, out_hbm, store_sem.at[0])
-    store_out.start()
-
-    if comm:
-        wait_all(spread_1)
-    total = part[...]
+        lax.fori_loop(5 * group, 5 * group + 5, body, 0, unroll=5)
+
+    read_back(0)
+    reduce_wait(0, gather_1)
+    row = part[my_row]
     for d in range(15):
-        total = total + gather_1[d]
-    total_1[...] = total
-    if comm:
-        start_all(spread_2)
+        row = row + gather_1[d]
+    row_sum[...] = row
+    reduce_send(1, peers_2, [row_sum] * 15, [gather_2.at[d] for d in range(15)])
+    read_back(1)
 
     for copy in copies_2:
         copy.wait()
+    reduce_wait(1, gather_2)
+    row = row_sum[...]
+    for d in range(15):
+        row = row + gather_2[d]
+    full[my_row] = row
+    reduce_send(2, peers_1, [full.at[my_row]] * 15, [full.at[my_row]] * 15)
     blank = jnp.zeros((CH, X), bf16)
 
     def clear(flag, places):
@@ -478,44 +485,70 @@
         group = i // 2
         half = slice(128 * (i % 2), 128 * (i % 2) + 128)
         table[16 * group : 16 * group + 16, half] = (result[i] / divisors[i]).astype(bf16)
-    read_back(grad_buf)
-    store_grad = pltpu.make_async_copy(grad_buf, grad_hbm, store_sem.at[1])
-    store_grad.start()
-
-    if comm:
-        wait_all(spread_2)
-    total = total_1[...]
-    for d in range(15):
-        total = total + gather_2[d]
+    reduce_wait(2, gather_1)
+    total = jnp.concatenate([full[i] for i in range(CH)], axis=0)
     total = (total * (1.0 / math.sqrt(CZ * CY * X * n_a * n_b))).T
     for i in range(27):
         wgrad_ref[i] = total[GRP * i : GRP * i + GRP]
+
+
+def last_kernel(
+    onehots, codes, table, out_buf, wgrad_ref, out_hbm, grad_hbm, wgrad_hbm, grad_buf, sem
+):
+    store_out = pltpu.make_async_copy(out_buf, out_hbm, sem.at[0])
+    store_weight = pltpu.make_async_copy(wgrad_ref, wgrad_hbm, sem.at[1])
+    store_out.start()
+    store_weight.start()
+
+    def store(group):
+        lanes = pl.ds(pl.multiple_of(group * (5 * S), 128), 5 * S)
+        return pltpu.make_async_copy(
+            grad_buf.at[:, lanes], grad_hbm.at[:, lanes], sem.at[2 + group]
+        )
+
+    def body(group, carry):
+        for j in range(5):
+            k = 5 * group + j
+            found = jnp.dot(table[...], onehots[k], preferred_element_type=f32)
+            grad_buf[:, pl.ds(pl.multiple_of(k * S, 128), S)] = select(found, codes[k])
+        store(group).start()
+        return carry
+
+    lax.fori_loop(0, 2, body, 0)
     store_out.wait()
-    store_grad.wait()
+    store_weight.wait()
+    store(0).wait()
+    store(1).wait()
 
 
 def fused(feats, cot, cells, slots, count, weight, comm=True):
-    hbm = pl.BlockSpec(memory_space=pl.ANY)
+    hbm = pl.BlockSpec(memory_space=pltpu.HBM)
     vmem = pl.BlockSpec(memory_space=pltpu.VMEM)
-    smem = pl.BlockSpec(memory_space=pltpu.SMEM)
     slots_all = ALL * S
     dma = pltpu.SemaphoreType.DMA
-    return pl.pallas_call(
+    shape = jax.ShapeDtypeStruct
+    feats, cot, cells, slots, count, weight = (
+        pltpu.with_memory_space_constraint(v, pltpu.HBM)
+        for v in (feats, cot, cells, slots, count, weight)
+    )
+    parts = pl.pallas_call(
         functools.partial(kernel, comm=comm),
         out_shape=[
-            jax.ShapeDtypeStruct((CH, slots_all), bf16),
-            jax.ShapeDtypeStruct((CH, slots_all), bf16),
-            jax.ShapeDtypeStruct((27, GRP, CH), f32),
+            shape((ALL, LO, S), bf16),
+            shape((ALL, 1, S), f32),
+            shape((128, LO), bf16),
+            shape((CH, slots_all), bf16),
+            shape((27, GRP, CH), f32),
         ],
-        in_specs=[hbm, hbm, vmem, vmem, smem, vmem],
-        out_specs=[hbm, hbm, vmem],
+        in_specs=[hbm] * 6,
+        out_specs=[vmem] * 5,
         scratch_shapes=[
             pltpu.VMEM((CH, OWN * S), bf16),
             pltpu.VMEM((CH, slots_all), bf16),
-            pltpu.VMEM((CH, slots_all), bf16),
-            pltpu.VMEM((CH, slots_all), bf16),
-            pltpu.VMEM((ALL, LO, S), bf16),
-            pltpu.VMEM((ALL, 1, S), f32),
+            pltpu.VMEM((112, 128), jnp.int32),
+            pltpu.VMEM((1, 2, S), jnp.int32),
+            pltpu.VMEM((1, 2), jnp.int32),
+            pltpu.VMEM((27, GRP, CH), bf16),
             pltpu.VMEM((OWN, 1, S), f32),
             pltpu.VMEM((272, LO), f32),
             pltpu.VMEM((128, LO), f32),
@@ -538,24 +571,36 @@
             pltpu.VMEM((48, 144), bf16),
             pltpu.VMEM((10, CH, 128), f32),
             pltpu.VMEM((48, CY * X), f32),
-            pltpu.VMEM((CH, 128), f32),
-            pltpu.VMEM((15, CH, 128), f32),
-            pltpu.VMEM((CH, 128), f32),
-            pltpu.VMEM((15, CH, 128), f32),
-            dma((2,)),
-            dma((2,)),
+            pltpu.VMEM((CH, 1, 128), f32),
+            pltpu.VMEM((15, 1, 128), f32),
+            pltpu.VMEM((1, 128), f32),
+            pltpu.VMEM((15, 1, 128), f32),
+            pltpu.VMEM((CH, 1, 128), f32),
+            dma((6,)),
             dma((10,)),
             dma((10,)),
             dma((8,)),
             dma((8,)),
-            dma((2, 15)),
-            dma((2, 15)),
+            dma((3,)),
+            dma((3,)),
         ],
         compiler_params=pltpu.CompilerParams(
-            vmem_limit_bytes=60 << 20,
+            vmem_limit_bytes=30 << 20,
             **(dict(collective_id=0, has_side_effects=True) if comm else {}),
         ),
     )(feats, cot, cells, slots, count, weight)
+    return pl.pallas_call(
+        last_kernel,
+        out_shape=[
+            shape((CH, slots_all), bf16),
+            shape((CH, slots_all), bf16),
+            shape((27, GRP, CH), f32),
+        ],
+        in_specs=[vmem] * 5,
+        out_specs=[hbm] * 3,
+        scratch_shapes=[pltpu.VMEM((CH, slots_all), bf16), dma((4,))],
+        compiler_params=pltpu.CompilerParams(vmem_limit_bytes=24 << 20),
+    )(*parts)
 
 
 def local(point_feats, cell_index, send_slots, send_count, conv_weight, point_cot):

time: 40.2 us -> 38.9 us (0.968)
  local copies, waits for them, and re-layouts: 3.43 us -> 0 us
  Pallas kernels: 35.9 us -> 38.2 us
    unnamed x7 -> x0, local copies, waits for them, and re-layouts: 3.43 us -> none
    pallas_call x1 -> x2, Pallas kernels: 35.9 us -> 38.2 us  [the longest x1 35.9 us: fused(): pl.pallas_call(functools.partial(kernel, comm=comm), out_shape=[shape((AL...]
where the time goes in v3:
time: 38.9 us; the launch traced here: 38.8 us
  Pallas kernels  38.2 us (98%)
  between operations  0.64 us (2%)
    pallas_call x1, Pallas kernels, fused(): pl.pallas_call(functools.partial(kernel, comm=comm), out_shape=[shape((AL...  35.9 us
    pallas_call x1, Pallas kernels, fused(): pl.pallas_call(last_kernel, out_shape=[shape((CH, slots_all), bf16), shap...  2.3 us

profile of v3, /device:TPU:1, one launch (start us, length us, event | category | flops | bytes accessed | tf_op | source)
XLA Modules:
  0.0 38.8 jit_solution(10248560602992551861)
XLA Ops:
  0.6 35.9 %shard_map.85 = (bf16[10,256,1792]{2,1,0:T(8,128)(2,1)S(1)}, f32[10,1,1792]{2,1,0:T(1,128)S(1)}, bf16[128,256]{1,0:T(8,128)(2,1)S(1)}, bf16[16,17920]{1,0:T(8,128)(2,1)S(1)}, f32[27,4,16]{2,1,0:T(4,128)S(1)}) custom-call(bf16[16,14336]{1,0:T(8,128)(2,1)} %feats_hbm.1, bf16[16,17920]{1,0:T(8,128)(2,1)} %cot_hbm.1, s32[112,128]{1,0:T(8,128)} %bitcast.7, ...), custom_call_target="tpu_custom_call" | custom-call | tf_op jit(solution)/shard_map/pallas_call | solution.py:534
  36.5 2.3 %shard_map.86 = (bf16[16,17920]{1,0:T(8,128)(2,1)}, bf16[16,17920]{1,0:T(8,128)(2,1)}, f32[27,4,16]{2,1,0:T(4,128)}) custom-call(bf16[10,256,1792]{2,1,0:T(8,128)(2,1)S(1)} %get-tuple-element.11.onehots, f32[10,1,1792]{2,1,0:T(1,128)S(1)} %get-tuple-element.12.codes, bf16[128,256]{1,0:T(8,128)(2,1)S(1)} %get-tuple-element.13.table, ...), custom_call_target="tpu_custom_call" | custom-call | tf_op jit(solution)/shard_map/pallas_call | solution.py:592

commit v4 on v3

--- a/solution.py
+++ b/solution.py
@@ -50,13 +50,13 @@
 
 def kernel(
     feats_hbm, cot_hbm, cells_hbm, slots_hbm, count_hbm, weight_hbm,
-    onehots, codes, table, out_buf, wgrad_ref,
-    feats, cot, cells_ref, slots_ref, count_ref, weight_ref, lows, acc, acc_cot,
+    out_buf, grad_buf, wgrad_ref,
+    onehots, codes, table, feats, cot, cells_ref, slots_ref, count_ref, weight_ref, lows, acc, acc_cot,
     list_send, list_recv,
     up_send, down_send, up_recv, down_recv,
     side_send, side_recv, corner_send, corner_recv,
     grid, gpad, patches, gp3, act, divisors, wmat, counts_in, pre,
-    part, gather_1, row_sum, gather_2, full,
+    part, gather_1, plane_sum, gather_2,
     load_sem, send_sem, recv_sem, send_2, recv_2, red_send, red_recv,
     *, comm,
 ):
@@ -83,14 +83,11 @@
 
     a_near = {-1: lax.rem(a + n_a - 1, n_a), 0: a, 1: lax.rem(a + 1, n_a)}
     b_all = [b] + [lax.rem(b + k, n_b) for k in range(1, 4)]
-    z_all = [z_p] + [lax.rem(z_p + k, 8) for k in range(1, 8)]
-    y_all = [y_p] + [lax.rem(y_p + k, 4) for k in range(1, 4)]
-    peers_1 = [(z_p * 8 + x_p + y_all[d // 4] * 2, b_all[d % 4]) for d in range(1, 16)]
-    rows_1 = [y_all[d // 4] * 4 + b_all[d % 4] for d in range(1, 16)]
-    peers_2 = [
-        (z_all[d // 2] * 8 + y_p * 2 + (1 - x_p if d % 2 else x_p), b) for d in range(1, 16)
+    plane_all = [
+        lax.rem(y_p + k // 2, 4) * 2 + (1 - x_p if k % 2 else x_p) for k in range(8)
     ]
-    my_row = y_p * 4 + b
+    peers_1 = [(z_p * 8 + plane_all[d // 4], b_all[d % 4]) for d in range(1, 32)]
+    peers_2 = [(lax.rem(z_p + k, 8) * 8 + plane_all[0], b) for k in range(1, 8)]
 
     def near(da, db):
         return (a_near[da], b_all[db % 4])
@@ -161,8 +158,7 @@
 
     counts = acc[256:272, :]
     count_hi = jnp.floor(counts * (1.0 / 256.0))
-    count_lo = (counts - 256.0 * count_hi).astype(bf16)
-    count_hi = count_hi.astype(bf16)
+    count_lo = counts - 256.0 * count_hi
 
     def block(number, row):
         lanes = slice(128 * (row % 2), 128 * (row % 2) + 128)
@@ -175,21 +171,22 @@
         for i, number in enumerate(members):
             ref[2 * i] = block(number, 0)
             ref[2 * i + 1] = block(number, 1)
-        ref[16] = count_lo[:, :128]
-        ref[17] = count_lo[:, 128:]
-        ref[18] = count_hi[:, :128]
-        ref[19] = count_hi[:, 128:]
+        both = jnp.concatenate(
+            [part_of[c : c + 4] for part_of in (count_lo, count_hi) for c in members[::4]], axis=0
+        ).astype(bf16)
+        ref[16] = both[:, :128]
+        ref[17] = both[:, 128:]
     for side in range(2):
         lanes = slice(128 * side, 128 * side + 128)
         for i, plane in enumerate(range(4)):
             side_send[side, i] = block(4 * plane + 3 * side, side)
-        side_send[side, 4] = count_lo[:, lanes]
-        side_send[side, 5] = count_hi[:, lanes]
+        side_send[side, 4] = count_lo[:, lanes].astype(bf16)
+        side_send[side, 5] = count_hi[:, lanes].astype(bf16)
         for vertical, planes in ((0, (0, 3)), (1, (1, 2))):
             for i, plane in enumerate(planes):
                 corner_send[2 * vertical + side, i] = block(4 * plane + 3 * side, side)
-            corner_send[2 * vertical + side, 2] = count_lo[:, lanes]
-            corner_send[2 * vertical + side, 3] = count_hi[:, lanes]
+            corner_send[2 * vertical + side, 2] = count_lo[:, lanes].astype(bf16)
+            corner_send[2 * vertical + side, 3] = count_hi[:, lanes].astype(bf16)
 
     copies = []
 
@@ -203,7 +200,7 @@
             copies.append(copy)
 
     if comm:
-        pl.semaphore_wait(barrier, len(around) + 30)
+        pl.semaphore_wait(barrier, len(around) + len(peers_1) + len(peers_2))
     send(list_send.at[0], list_recv.at[1], 0, -1, 0)
     send(list_send.at[1], list_recv.at[0], 1, 1, 0)
     send(up_send, up_recv, 2, 1, 0)
@@ -265,14 +262,10 @@
     has_left = b > 0
     has_right = b < n_b - 1
 
-    def unpack(ref, at, flag):
-        total = ref[at + 1].astype(f32) * 256.0 + ref[at].astype(f32)
-        return jnp.where(flag, total, 0.0)
-
     for i, (ref, flag) in enumerate(((up_recv, has_below), (down_recv, has_above))):
         for half in range(2):
-            total = ref[18 + half].astype(f32) * 256.0 + ref[16 + half].astype(f32)
-            counts_in[2 * i + half] = jnp.where(flag, total, 0.0)
+            both = ref[16 + half].astype(f32)
+            counts_in[2 * i + half, 0:8] = jnp.where(flag, both[0:8] + 256.0 * both[8:16], 0.0)
     side_flag = (has_right, has_left)
     for side in range(2):
         for i, (ref, at) in enumerate(
@@ -290,17 +283,17 @@
         return sums / jnp.maximum(count, 1.0)
 
     sources = (
-        (3, up_recv, 4, 2, 0, has_below),
-        (0, up_recv, 0, 1, 0, has_below),
-        (2, down_recv, 4, 3, 2, has_above),
-        (1, down_recv, 0, 0, 2, has_above),
+        (3, up_recv, 4, 0, has_below),
+        (0, up_recv, 0, 0, has_below),
+        (2, down_recv, 4, 2, has_above),
+        (1, down_recv, 0, 2, has_above),
     )
-    for plane, (mine, ref, at, theirs, where, flag) in enumerate(sources):
+    for plane, (mine, ref, at, where, flag) in enumerate(sources):
         for row in range(8):
             half = row % 2
             lanes = slice(128 * half, 128 * half + 128)
             number = 4 * mine + row // 2
-            other = 4 * theirs + row // 2
+            other = at + row // 2
             got = ref[2 * (at + row // 2) + half].astype(f32)
             sums = acc[16 * number : 16 * number + 16, lanes] + jnp.where(flag, got, 0.0)
             count = acc[256 + number : 257 + number, lanes]
@@ -360,26 +353,6 @@
             cot_sum = acc_cot[16 * group : 16 * group + 16, half]
             gpad[z + 1, y + 1] = (cot_sum * sigma * (1.0 + value * (1.0 - sigma))).astype(bf16)
 
-    copies_2 = []
-
-    def send_2nd(src, dst, place, da, db):
-        if comm:
-            copy = pltpu.make_async_remote_copy(
-                src_ref=src, dst_ref=dst, send_sem=send_2.at[place],
-                recv_sem=recv_2.at[place], device_id=near(da, db), device_id_type=MESH,
-            )
-            copy.start()
-            copies_2.append(copy)
-
-    send_2nd(gpad.at[1, pl.ds(1, 8)], gpad.at[3, pl.ds(1, 8)], 0, -1, 0)
-    send_2nd(gpad.at[2, pl.ds(1, 8)], gpad.at[0, pl.ds(1, 8)], 1, 1, 0)
-    send_2nd(gpad.at[pl.ds(1, 2), 1], gpad.at[pl.ds(1, 2), 9], 2, 0, -1)
-    send_2nd(gpad.at[pl.ds(1, 2), 8], gpad.at[pl.ds(1, 2), 0], 3, 0, 1)
-    send_2nd(gpad.at[1, 1], gpad.at[3, 9], 4, -1, -1)
-    send_2nd(gpad.at[1, 8], gpad.at[3, 0], 5, -1, 1)
-    send_2nd(gpad.at[2, 1], gpad.at[0, 9], 6, 1, -1)
-    send_2nd(gpad.at[2, 8], gpad.at[0, 0], 7, 1, 1)
-
     def move(plane, row):
         value = gpad[plane, row]
         wide = value.astype(f32)
@@ -405,14 +378,13 @@
             preferred_element_type=f32,
         )
         compact += picked[0:16] + picked[16:32] + picked[32:48]
-    for i in range(CH):
-        part[i] = compact[i : i + 1]
-
-    def reduce_send(step, peers, sources, targets):
+    part[...] = compact.astype(bf16)
+
+    def reduce_send(step, peers, source, target):
         if comm:
-            for place, src, dst in zip(peers, sources, targets):
+            for d, place in enumerate(peers):
                 pltpu.make_async_remote_copy(
-                    src_ref=src, dst_ref=dst, send_sem=red_send.at[step],
+                    src_ref=source, dst_ref=target.at[d], send_sem=red_send.at[step],
                     recv_sem=red_recv.at[step], device_id=place, device_id_type=MESH,
                 ).start()
 
@@ -421,33 +393,40 @@
             pltpu.make_async_copy(buffer, buffer, red_send.at[step]).wait()
             pltpu.make_async_copy(buffer, buffer, red_recv.at[step]).wait()
 
-    reduce_send(0, peers_1, [part.at[r] for r in rows_1], [gather_1.at[d] for d in range(15)])
-
-    def read_back(group):
+    reduce_send(0, peers_1, part, gather_1)
+    copies_2 = []
+
+    def send_2nd(src, dst, place, da, db):
+        if comm:
+            copy = pltpu.make_async_remote_copy(
+                src_ref=src, dst_ref=dst, send_sem=send_2.at[place],
+                recv_sem=recv_2.at[place], device_id=near(da, db), device_id_type=MESH,
+            )
+            copy.start()
+            copies_2.append(copy)
+
+    send_2nd(gpad.at[1, pl.ds(1, 8)], gpad.at[3, pl.ds(1, 8)], 0, -1, 0)
+    send_2nd(gpad.at[2, pl.ds(1, 8)], gpad.at[0, pl.ds(1, 8)], 1, 1, 0)
+    send_2nd(gpad.at[pl.ds(1, 2), 1], gpad.at[pl.ds(1, 2), 9], 2, 0, -1)
+    send_2nd(gpad.at[pl.ds(1, 2), 8], gpad.at[pl.ds(1, 2), 0], 3, 0, 1)
+    send_2nd(gpad.at[1, 1], gpad.at[3, 9], 4, -1, -1)
+    send_2nd(gpad.at[1, 8], gpad.at[3, 0], 5, -1, 1)
+    send_2nd(gpad.at[2, 1], gpad.at[0, 9], 6, 1, -1)
+    send_2nd(gpad.at[2, 8], gpad.at[0, 0], 7, 1, 1)
+
+
+    def read_back(values, into):
         def body(k, carry):
-            found = jnp.dot(act[...], onehots[k], preferred_element_type=f32)
-            out_buf[:, pl.ds(pl.multiple_of(k * S, 128), S)] = select(found, codes[k])
+            found = jnp.dot(values[...], onehots[k], preferred_element_type=f32)
+            into[:, pl.ds(pl.multiple_of(k * S, 128), S)] = select(found, codes[k])
             return carry
 
-        lax.fori_loop(5 * group, 5 * group + 5, body, 0, unroll=5)
-
-    read_back(0)
-    reduce_wait(0, gather_1)
-    row = part[my_row]
-    for d in range(15):
-        row = row + gather_1[d]
-    row_sum[...] = row
-    reduce_send(1, peers_2, [row_sum] * 15, [gather_2.at[d] for d in range(15)])
-    read_back(1)
+        lax.fori_loop(0, ALL, body, 0, unroll=5)
+
+    read_back(act, out_buf)
 
     for copy in copies_2:
         copy.wait()
-    reduce_wait(1, gather_2)
-    row = row_sum[...]
-    for d in range(15):
-        row = row + gather_2[d]
-    full[my_row] = row
-    reduce_send(2, peers_1, [full.at[my_row]] * 15, [full.at[my_row]] * 15)
     blank = jnp.zeros((CH, X), bf16)
 
     def clear(flag, places):
@@ -485,40 +464,33 @@
         group = i // 2
         half = slice(128 * (i % 2), 128 * (i % 2) + 128)
         table[16 * group : 16 * group + 16, half] = (result[i] / divisors[i]).astype(bf16)
-    reduce_wait(2, gather_1)
-    total = jnp.concatenate([full[i] for i in range(CH)], axis=0)
+    reduce_wait(0, gather_1)
+    total = compact
+    for d in range(31):
+        total = total + gather_1[d].astype(f32)
+    plane_sum[...] = total.astype(bf16)
+    reduce_send(1, peers_2, plane_sum, gather_2)
+
+    read_back(table, grad_buf)
+
+    reduce_wait(1, gather_2)
+    for d in range(7):
+        total = total + gather_2[d].astype(f32)
     total = (total * (1.0 / math.sqrt(CZ * CY * X * n_a * n_b))).T
     for i in range(27):
         wgrad_ref[i] = total[GRP * i : GRP * i + GRP]
 
 
-def last_kernel(
-    onehots, codes, table, out_buf, wgrad_ref, out_hbm, grad_hbm, wgrad_hbm, grad_buf, sem
-):
-    store_out = pltpu.make_async_copy(out_buf, out_hbm, sem.at[0])
-    store_weight = pltpu.make_async_copy(wgrad_ref, wgrad_hbm, sem.at[1])
-    store_out.start()
-    store_weight.start()
-
-    def store(group):
-        lanes = pl.ds(pl.multiple_of(group * (5 * S), 128), 5 * S)
-        return pltpu.make_async_copy(
-            grad_buf.at[:, lanes], grad_hbm.at[:, lanes], sem.at[2 + group]
-        )
-
-    def body(group, carry):
-        for j in range(5):
-            k = 5 * group + j
-            found = jnp.dot(table[...], onehots[k], preferred_element_type=f32)
-            grad_buf[:, pl.ds(pl.multiple_of(k * S, 128), S)] = select(found, codes[k])
-        store(group).start()
-        return carry
-
-    lax.fori_loop(0, 2, body, 0)
-    store_out.wait()
-    store_weight.wait()
-    store(0).wait()
-    store(1).wait()
+def copy_kernel(*refs):
+    sources, targets, sem = refs[:3], refs[3:6], refs[6]
+    copies = [
+        pltpu.make_async_copy(src, dst, sem.at[i])
+        for i, (src, dst) in enumerate(zip(sources, targets))
+    ]
+    for copy in copies:
+        copy.start()
+    for copy in copies:
+        copy.wait()
 
 
 def fused(feats, cot, cells, slots, count, weight, comm=True):
@@ -534,15 +506,16 @@
     parts = pl.pallas_call(
         functools.partial(kernel, comm=comm),
         out_shape=[
-            shape((ALL, LO, S), bf16),
-            shape((ALL, 1, S), f32),
-            shape((128, LO), bf16),
+            shape((CH, slots_all), bf16),
             shape((CH, slots_all), bf16),
             shape((27, GRP, CH), f32),
         ],
         in_specs=[hbm] * 6,
-        out_specs=[vmem] * 5,
+        out_specs=[vmem] * 3,
         scratch_shapes=[
+            pltpu.VMEM((ALL, LO, S), bf16),
+            pltpu.VMEM((ALL, 1, S), f32),
+            pltpu.VMEM((128, LO), bf16),
             pltpu.VMEM((CH, OWN * S), bf16),
             pltpu.VMEM((CH, slots_all), bf16),
             pltpu.VMEM((112, 128), jnp.int32),
@@ -554,10 +527,10 @@
             pltpu.VMEM((128, LO), f32),
             pltpu.VMEM((2, 1, S), f32),
             pltpu.VMEM((2, 1, S), f32),
-            pltpu.VMEM((20, CH, 128), bf16),
-            pltpu.VMEM((20, CH, 128), bf16),
-            pltpu.VMEM((20, CH, 128), bf16),
-            pltpu.VMEM((20, CH, 128), bf16),
+            pltpu.VMEM((18, CH, 128), bf16),
+            pltpu.VMEM((18, CH, 128), bf16),
+            pltpu.VMEM((18, CH, 128), bf16),
+            pltpu.VMEM((18, CH, 128), bf16),
             pltpu.VMEM((2, 6, CH, 128), bf16),
             pltpu.VMEM((2, 6, CH, 128), bf16),
             pltpu.VMEM((4, 4, CH, 128), bf16),
@@ -571,18 +544,17 @@
             pltpu.VMEM((48, 144), bf16),
             pltpu.VMEM((10, CH, 128), f32),
             pltpu.VMEM((48, CY * X), f32),
-            pltpu.VMEM((CH, 1, 128), f32),
-            pltpu.VMEM((15, 1, 128), f32),
-            pltpu.VMEM((1, 128), f32),
-            pltpu.VMEM((15, 1, 128), f32),
-            pltpu.VMEM((CH, 1, 128), f32),
+            pltpu.VMEM((CH, 128), bf16),
+            pltpu.VMEM((31, CH, 128), bf16),
+            pltpu.VMEM((CH, 128), bf16),
+            pltpu.VMEM((7, CH, 128), bf16),
             dma((6,)),
             dma((10,)),
             dma((10,)),
             dma((8,)),
             dma((8,)),
-            dma((3,)),
-            dma((3,)),
+            dma((2,)),
+            dma((2,)),
         ],
         compiler_params=pltpu.CompilerParams(
             vmem_limit_bytes=30 << 20,
@@ -590,17 +562,16 @@
         ),
     )(feats, cot, cells, slots, count, weight)
     return pl.pallas_call(
-        last_kernel,
+        copy_kernel,
         out_shape=[
             shape((CH, slots_all), bf16),
             shape((CH, slots_all), bf16),
             shape((27, GRP, CH), f32),
         ],
-        in_specs=[vmem] * 5,
+        in_specs=[vmem] * 3,
         out_specs=[hbm] * 3,
-        scratch_shapes=[pltpu.VMEM((CH, slots_all), bf16), dma((4,))],
-        compiler_params=pltpu.CompilerParams(vmem_limit_bytes=24 << 20),
-    )(*parts)
+        scratch_shapes=[dma((3,))],
+    )(*(pltpu.with_memory_space_constraint(v, pltpu.VMEM) for v in parts))
 
 
 def local(point_feats, cell_index, send_slots, send_count, conv_weight, point_cot):

time: 38.9 us -> 32.3 us (0.83)
  Pallas kernels: 38.2 us -> 31.6 us
    pallas_call x2, Pallas kernels: 38.2 us -> 31.6 us  [the longest x1 30.6 us: fused(): pl.pallas_call(functools.partial(kernel, comm=comm), out_shape=[shape((CH...]
where the time goes in v4:
time: 32.3 us; the launch traced here: 32.2 us
  Pallas kernels  31.6 us (98%)
  between operations  0.64 us (2%)
    pallas_call x1, Pallas kernels, fused(): pl.pallas_call(functools.partial(kernel, comm=comm), out_shape=[shape((CH...  30.6 us
    pallas_call x1, Pallas kernels, fused(): pl.pallas_call(copy_kernel, out_shape=[shape((CH, slots_all), bf16), shap...  1.03 us

profile of v4, /device:TPU:1, one launch (start us, length us, event | category | flops | bytes accessed | tf_op | source)
XLA Modules:
  0.0 32.2 jit_solution(807347783245388036)
XLA Ops:
  0.6 30.6 %shard_map.85 = (bf16[16,17920]{1,0:T(8,128)(2,1)S(1)}, bf16[16,17920]{1,0:T(8,128)(2,1)S(1)}, f32[27,4,16]{2,1,0:T(4,128)S(1)}) custom-call(bf16[16,14336]{1,0:T(8,128)(2,1)} %feats_hbm.1, bf16[16,17920]{1,0:T(8,128)(2,1)} %cot_hbm.1, s32[112,128]{1,0:T(8,128)} %bitcast.7, s32[1,2,1792]{2,1,0:T(2,128)} %slots_hbm.1, s32[1,2]{1,0:T(1,128)} %count_hbm.1, ...), custom_call_target="tpu_custom_call" | custom-call | tf_op jit(solution)/shard_map/pallas_call | solution.py:506
  31.2 1.0 %shard_map.86 = (bf16[16,17920]{1,0:T(8,128)(2,1)}, bf16[16,17920]{1,0:T(8,128)(2,1)}, f32[27,4,16]{2,1,0:T(4,128)}) custom-call(bf16[16,17920]{1,0:T(8,128)(2,1)S(1)} %get-tuple-element.9.refs_0_, bf16[16,17920]{1,0:T(8,128)(2,1)S(1)} %get-tuple-element.10.refs_1_, f32[27,4,16]{2,1,0:T(4,128)S(1)} %get-tuple-element.11.refs_2_), custom_call_target="tpu_custom_call" | custom-call | tf_op jit(solution)/shard_map/pallas_call | solution.py:564

commit v5 on v4

--- a/solution.py
+++ b/solution.py
@@ -176,41 +176,73 @@
         ).astype(bf16)
         ref[16] = both[:, :128]
         ref[17] = both[:, 128:]
+    nothing = jnp.zeros((8, 128), f32)
     for side in range(2):
         lanes = slice(128 * side, 128 * side + 128)
-        for i, plane in enumerate(range(4)):
-            side_send[side, i] = block(4 * plane + 3 * side, side)
-        side_send[side, 4] = count_lo[:, lanes].astype(bf16)
-        side_send[side, 5] = count_hi[:, lanes].astype(bf16)
+        rows = [
+            part_of[4 * plane + 3 * side : 4 * plane + 3 * side + 1, lanes]
+            for part_of in (count_lo, count_hi)
+            for plane in range(4)
+        ]
+        tile = jnp.concatenate(rows + [nothing], axis=0).astype(bf16)
+        for plane in range(4):
+            side_send[side, plane] = block(4 * plane + 3 * side, side)
+        side_send[side, 4] = tile
         for vertical, planes in ((0, (0, 3)), (1, (1, 2))):
             for i, plane in enumerate(planes):
                 corner_send[2 * vertical + side, i] = block(4 * plane + 3 * side, side)
-            corner_send[2 * vertical + side, 2] = count_lo[:, lanes].astype(bf16)
-            corner_send[2 * vertical + side, 3] = count_hi[:, lanes].astype(bf16)
-
-    copies = []
-
-    def send(src, dst, place, da, db):
-        if comm:
-            copy = pltpu.make_async_remote_copy(
-                src_ref=src, dst_ref=dst, send_sem=send_sem.at[place],
-                recv_sem=recv_sem.at[place], device_id=near(da, db), device_id_type=MESH,
-            )
+            corner_send[2 * vertical + side, 2] = tile
+
+    def inside(da, db):
+        tests = []
+        if da:
+            tests.append(a < n_a - 1 if da > 0 else a > 0)
+        if db:
+            tests.append(b < n_b - 1 if db > 0 else b > 0)
+        return tests[0] if len(tests) == 1 else jnp.logical_and(*tests)
+
+    def send(src, dst, sems, place, da, db):
+        if not comm:
+            return lambda: None
+        copy = pltpu.make_async_remote_copy(
+            src_ref=src, dst_ref=dst, send_sem=sems[0].at[place],
+            recv_sem=sems[1].at[place], device_id=near(da, db), device_id_type=MESH,
+        )
+
+        @pl.when(inside(da, db))
+        def _():
             copy.start()
-            copies.append(copy)
+
+        def finish():
+            @pl.when(inside(da, db))
+            def _():
+                copy.wait_send()
+
+            @pl.when(inside(-da, -db))
+            def _():
+                copy.wait_recv()
+
+        return finish
 
     if comm:
         pl.semaphore_wait(barrier, len(around) + len(peers_1) + len(peers_2))
-    send(list_send.at[0], list_recv.at[1], 0, -1, 0)
-    send(list_send.at[1], list_recv.at[0], 1, 1, 0)
-    send(up_send, up_recv, 2, 1, 0)
-    send(down_send, down_recv, 3, -1, 0)
+    first = (send_sem, recv_sem)
+    finish_lists = [
+        send(list_send.at[0], list_recv.at[1], first, 0, -1, 0),
+        send(list_send.at[1], list_recv.at[0], first, 1, 1, 0),
+    ]
+    finish_grid = [
+        send(up_send, up_recv, first, 2, 1, 0),
+        send(down_send, down_recv, first, 3, -1, 0),
+    ]
     for side in range(2):
         db = 2 * side - 1
-        send(side_send.at[side], side_recv.at[side], 4 + side, 0, db)
+        finish_grid.append(send(side_send.at[side], side_recv.at[side], first, 4 + side, 0, db))
         for vertical in range(2):
             i = 2 * vertical + side
-            send(corner_send.at[i], corner_recv.at[i], 6 + i, 2 * vertical - 1, db)
+            finish_grid.append(
+                send(corner_send.at[i], corner_recv.at[i], first, 6 + i, 2 * vertical - 1, db)
+            )
 
     load_weight.wait()
     weight = jnp.concatenate(
@@ -236,9 +268,8 @@
 
     lax.fori_loop(0, OWN, splat_cot, 0, unroll=4)
 
-    if comm:
-        copies[0].wait()
-        copies[1].wait()
+    for finish in finish_lists:
+        finish()
     for side in range(2):
         present = (a > 0) if side == 0 else (a < n_a - 1)
         place = jnp.where(present, list_recv[side], -1.0).astype(jnp.int32)
@@ -254,9 +285,8 @@
             preferred_element_type=f32,
         )
 
-    if comm:
-        for copy in copies[2:]:
-            copy.wait()
+    for finish in finish_grid:
+        finish()
     has_below = a > 0
     has_above = a < n_a - 1
     has_left = b > 0
@@ -276,8 +306,8 @@
                 flag = jnp.logical_and(flag, has_above)
             if i == 2:
                 flag = jnp.logical_and(flag, has_below)
-            total = ref[at + 1].astype(f32) * 256.0 + ref[at].astype(f32)
-            counts_in[(4 if i == 0 else 4 + 2 * i) + side] = jnp.where(flag, total, 0.0)
+            both = ref[at].astype(f32)
+            counts_in[4 + 2 * i + side, 0:4] = jnp.where(flag, both[0:4] + 256.0 * both[4:8], 0.0)
 
     def mean(sums, count):
         return sums / jnp.maximum(count, 1.0)
@@ -304,7 +334,6 @@
                 divisors[8 * (plane - 1) + row] = divisor
     for side in range(2):
         flag = side_flag[side]
-        y_hi = 3 * side
         halo = (
             (3, 1, 1, 2, has_below),
             (0, 1, 0, 1, has_below),
@@ -316,11 +345,9 @@
             both = jnp.logical_and(flag, vertical_flag)
             sums = jnp.where(flag, side_recv[side, direct].astype(f32), 0.0)
             sums = sums + jnp.where(both, corner_recv[corner, at].astype(f32), 0.0)
-            mine = 4 * direct + y_hi
-            other = 4 * theirs + y_hi
             kind = 6 if vertical == 0 else 8
-            count = counts_in[4 + side, mine : mine + 1, :]
-            count = count + counts_in[kind + side, other : other + 1, :]
+            count = counts_in[4 + side, direct : direct + 1, :]
+            count = count + counts_in[kind + side, theirs : theirs + 1, :]
             grid[plane, 9 * (1 - side)] = mean(sums, count).astype(bf16)
 
     lane = lax.broadcasted_iota(jnp.int32, (CH, X), 1)
@@ -369,15 +396,9 @@
     compact = jnp.zeros((CH, 128), f32)
     for col_k in range(3):
         kept = jnp.where(same_group, wide_grad[16 * col_k : 16 * col_k + 16], 0.0)
-        first = kept.astype(bf16)
-        rest = kept - first.astype(f32)
-        second = rest.astype(bf16)
-        third = (rest - second.astype(f32)).astype(bf16)
-        picked = jnp.dot(
-            jnp.concatenate([first, second, third], axis=0), spread[col_k].astype(bf16),
-            preferred_element_type=f32,
-        )
-        compact += picked[0:16] + picked[16:32] + picked[32:48]
+        compact += jnp.dot(
+            kept.astype(bf16), spread[col_k].astype(bf16), preferred_element_type=f32
+        )
     part[...] = compact.astype(bf16)
 
     def reduce_send(step, peers, source, target):
@@ -394,16 +415,11 @@
             pltpu.make_async_copy(buffer, buffer, red_recv.at[step]).wait()
 
     reduce_send(0, peers_1, part, gather_1)
-    copies_2 = []
+    second = (send_2, recv_2)
+    finish_halo = []
 
     def send_2nd(src, dst, place, da, db):
-        if comm:
-            copy = pltpu.make_async_remote_copy(
-                src_ref=src, dst_ref=dst, send_sem=send_2.at[place],
-                recv_sem=recv_2.at[place], device_id=near(da, db), device_id_type=MESH,
-            )
-            copy.start()
-            copies_2.append(copy)
+        finish_halo.append(send(src, dst, second, place, da, db))
 
     send_2nd(gpad.at[1, pl.ds(1, 8)], gpad.at[3, pl.ds(1, 8)], 0, -1, 0)
     send_2nd(gpad.at[2, pl.ds(1, 8)], gpad.at[0, pl.ds(1, 8)], 1, 1, 0)
@@ -425,8 +441,8 @@
 
     read_back(act, out_buf)
 
-    for copy in copies_2:
-        copy.wait()
+    for finish in finish_halo:
+        finish()
     blank = jnp.zeros((CH, X), bf16)
 
     def clear(flag, places):
@@ -531,10 +547,10 @@
             pltpu.VMEM((18, CH, 128), bf16),
             pltpu.VMEM((18, CH, 128), bf16),
             pltpu.VMEM((18, CH, 128), bf16),
-            pltpu.VMEM((2, 6, CH, 128), bf16),
-            pltpu.VMEM((2, 6, CH, 128), bf16),
-            pltpu.VMEM((4, 4, CH, 128), bf16),
-            pltpu.VMEM((4, 4, CH, 128), bf16),
+            pltpu.VMEM((2, 5, CH, 128), bf16),
+            pltpu.VMEM((2, 5, CH, 128), bf16),
+            pltpu.VMEM((4, 3, CH, 128), bf16),
+            pltpu.VMEM((4, 3, CH, 128), bf16),
             pltpu.VMEM((4, 10, CH, 128), bf16),
             pltpu.VMEM((4, 10, CH, 128), bf16),
             pltpu.VMEM((CZ, 144, CY * X), bf16),

time: 32.3 us -> 32.3 us (level)
  no operation moved by 1% of the time
where the time goes in v5:
time: 32.3 us; the launch traced here: 32.2 us
  Pallas kernels  31.6 us (98%)
  between operations  0.64 us (2%)
    pallas_call x1, Pallas kernels, fused(): pl.pallas_call(functools.partial(kernel, comm=comm), out_shape=[shape((CH...  30.5 us
    pallas_call x1, Pallas kernels, fused(): pl.pallas_call(copy_kernel, out_shape=[shape((CH, slots_all), bf16), shap...  1.03 us

profile of v5, /device:TPU:1, one launch (start us, length us, event | category | flops | bytes accessed | tf_op | source)
XLA Modules:
  0.0 32.2 jit_solution(6805459763839089073)
XLA Ops:
  0.6 30.5 %shard_map.85 = (bf16[16,17920]{1,0:T(8,128)(2,1)S(1)}, bf16[16,17920]{1,0:T(8,128)(2,1)S(1)}, f32[27,4,16]{2,1,0:T(4,128)S(1)}) custom-call(bf16[16,14336]{1,0:T(8,128)(2,1)} %feats_hbm.1, bf16[16,17920]{1,0:T(8,128)(2,1)} %cot_hbm.1, s32[112,128]{1,0:T(8,128)} %bitcast.7, s32[1,2,1792]{2,1,0:T(2,128)} %slots_hbm.1, s32[1,2]{1,0:T(1,128)} %count_hbm.1, ...), custom_call_target="tpu_custom_call" | custom-call | tf_op jit(solution)/shard_map/pallas_call | solution.py:522
  31.2 1.0 %shard_map.86 = (bf16[16,17920]{1,0:T(8,128)(2,1)}, bf16[16,17920]{1,0:T(8,128)(2,1)}, f32[27,4,16]{2,1,0:T(4,128)}) custom-call(bf16[16,17920]{1,0:T(8,128)(2,1)S(1)} %get-tuple-element.9.refs_0_, bf16[16,17920]{1,0:T(8,128)(2,1)S(1)} %get-tuple-element.10.refs_1_, f32[27,4,16]{2,1,0:T(4,128)S(1)} %get-tuple-element.11.refs_2_), custom_call_target="tpu_custom_call" | custom-call | tf_op jit(solution)/shard_map/pallas_call | solution.py:580

commit v6 on v5

--- a/solution.py
+++ b/solution.py
@@ -441,6 +441,13 @@
 
     read_back(act, out_buf)
 
+    reduce_wait(0, gather_1)
+    total = compact
+    for d in range(31):
+        total = total + gather_1[d].astype(f32)
+    plane_sum[...] = total.astype(bf16)
+    reduce_send(1, peers_2, plane_sum, gather_2)
+
     for finish in finish_halo:
         finish()
     blank = jnp.zeros((CH, X), bf16)
@@ -480,31 +487,25 @@
         group = i // 2
         half = slice(128 * (i % 2), 128 * (i % 2) + 128)
         table[16 * group : 16 * group + 16, half] = (result[i] / divisors[i]).astype(bf16)
-    reduce_wait(0, gather_1)
-    total = compact
-    for d in range(31):
-        total = total + gather_1[d].astype(f32)
-    plane_sum[...] = total.astype(bf16)
-    reduce_send(1, peers_2, plane_sum, gather_2)
-
     read_back(table, grad_buf)
 
     reduce_wait(1, gather_2)
     for d in range(7):
         total = total + gather_2[d].astype(f32)
-    total = (total * (1.0 / math.sqrt(CZ * CY * X * n_a * n_b))).T
-    for i in range(27):
-        wgrad_ref[i] = total[GRP * i : GRP * i + GRP]
-
-
-def copy_kernel(*refs):
-    sources, targets, sem = refs[:3], refs[3:6], refs[6]
+    wgrad_ref[...] = total * (1.0 / math.sqrt(CZ * CY * X * n_a * n_b))
+
+
+def copy_kernel(out, grad, total, out_hbm, grad_hbm, wgrad_hbm, wgrad, sem):
     copies = [
         pltpu.make_async_copy(src, dst, sem.at[i])
-        for i, (src, dst) in enumerate(zip(sources, targets))
+        for i, (src, dst) in enumerate(((out, out_hbm), (grad, grad_hbm), (wgrad, wgrad_hbm)))
     ]
-    for copy in copies:
-        copy.start()
+    copies[0].start()
+    copies[1].start()
+    turned = total[...].T
+    for i in range(27):
+        wgrad[i] = turned[GRP * i : GRP * i + GRP]
+    copies[2].start()
     for copy in copies:
         copy.wait()
 
@@ -524,7 +525,7 @@
         out_shape=[
             shape((CH, slots_all), bf16),
             shape((CH, slots_all), bf16),
-            shape((27, GRP, CH), f32),
+            shape((CH, 128), f32),
         ],
         in_specs=[hbm] * 6,
         out_specs=[vmem] * 3,
@@ -586,7 +587,7 @@
         ],
         in_specs=[vmem] * 3,
         out_specs=[hbm] * 3,
-        scratch_shapes=[dma((3,))],
+        scratch_shapes=[pltpu.VMEM((27, GRP, CH), f32), dma((3,))],
     )(*(pltpu.with_memory_space_constraint(v, pltpu.VMEM) for v in parts))
 
 

time: 32.3 us -> 31.6 us (0.978)
  Pallas kernels: 31.6 us -> 30.8 us
    pallas_call x1, Pallas kernels: 30.5 us -> 29.8 us  [fused(): pl.pallas_call(functools.partial(kernel, comm=comm), out_shape=[shape((CH...]
where the time goes in v6:
time: 31.6 us; the launch traced here: 31.5 us
  Pallas kernels  30.8 us (97%)
  between operations  0.64 us (2%)
    pallas_call x1, Pallas kernels, fused(): pl.pallas_call(functools.partial(kernel, comm=comm), out_shape=[shape((CH...  29.8 us
    pallas_call x1, Pallas kernels, fused(): pl.pallas_call(copy_kernel, out_shape=[shape((CH, slots_all), bf16), shap...  1.03 us

profile of v6, /device:TPU:1, one launch (start us, length us, event | category | flops | bytes accessed | tf_op | source)
XLA Modules:
  0.0 31.5 jit_solution(3364726126678410455)
XLA Ops:
  0.6 29.8 %shard_map.85 = (bf16[16,17920]{1,0:T(8,128)(2,1)S(1)}, bf16[16,17920]{1,0:T(8,128)(2,1)S(1)}, f32[16,128]{1,0:T(8,128)S(1)}) custom-call(bf16[16,14336]{1,0:T(8,128)(2,1)} %feats_hbm.1, bf16[16,17920]{1,0:T(8,128)(2,1)} %cot_hbm.1, s32[112,128]{1,0:T(8,128)} %bitcast.7, s32[1,2,1792]{2,1,0:T(2,128)} %slots_hbm.1, s32[1,2]{1,0:T(1,128)} %count_hbm.1, ...), custom_call_target="tpu_custom_call" | custom-call | tf_op jit(solution)/shard_map/pallas_call | solution.py:523
  30.4 1.0 %shard_map.86 = (bf16[16,17920]{1,0:T(8,128)(2,1)}, bf16[16,17920]{1,0:T(8,128)(2,1)}, f32[27,4,16]{2,1,0:T(4,128)}) custom-call(bf16[16,17920]{1,0:T(8,128)(2,1)S(1)} %get-tuple-element.9.out, bf16[16,17920]{1,0:T(8,128)(2,1)S(1)} %get-tuple-element.10.grad, f32[16,128]{1,0:T(8,128)S(1)} %get-tuple-element.11.total), custom_call_target="tpu_custom_call" | custom-call | tf_op jit(solution)/shard_map/pallas_call | solution.py:581

commit v7 on v6

--- a/solution.py
+++ b/solution.py
@@ -25,6 +25,14 @@
 UP_MSG = tuple(range(4, 12))
 DOWN_MSG = (0, 1, 2, 3, 12, 13, 14, 15)
 STAY = (0, 1, 2, 3, 8, 9, 10, 11)
+
+
+def links(d):
+    step_y, step_x, step_b = (0, 1, 2, 1)[d // 8], d // 4 % 2, d % 4
+    return step_y + (2 - step_x if step_b == 2 else max(step_x, step_b % 2))
+
+
+FAR_FIRST = sorted(range(1, 32), key=links, reverse=True)
 
 
 def one_hot(row, count):
@@ -86,8 +94,8 @@
     plane_all = [
         lax.rem(y_p + k // 2, 4) * 2 + (1 - x_p if k % 2 else x_p) for k in range(8)
     ]
-    peers_1 = [(z_p * 8 + plane_all[d // 4], b_all[d % 4]) for d in range(1, 32)]
-    peers_2 = [(lax.rem(z_p + k, 8) * 8 + plane_all[0], b) for k in range(1, 8)]
+    peers_1 = [(z_p * 8 + plane_all[d // 4], b_all[d % 4]) for d in FAR_FIRST]
+    peers_2 = [(lax.rem(z_p + k, 8) * 8 + plane_all[0], b) for k in (4, 3, 5, 2, 6, 1, 7)]
 
     def near(da, db):
         return (a_near[da], b_all[db % 4])
@@ -201,6 +209,8 @@
             tests.append(b < n_b - 1 if db > 0 else b > 0)
         return tests[0] if len(tests) == 1 else jnp.logical_and(*tests)
 
+    wait_sent = []
+
     def send(src, dst, sems, place, da, db):
         if not comm:
             return lambda: None
@@ -213,14 +223,17 @@
         def _():
             copy.start()
 
-        def finish():
+        def sent():
             @pl.when(inside(da, db))
             def _():
                 copy.wait_send()
 
+        def finish():
             @pl.when(inside(-da, -db))
             def _():
                 copy.wait_recv()
+
+        wait_sent.append(sent)
 
         return finish
 
@@ -411,8 +424,8 @@
 
     def reduce_wait(step, buffer):
         if comm:
-            pltpu.make_async_copy(buffer, buffer, red_send.at[step]).wait()
             pltpu.make_async_copy(buffer, buffer, red_recv.at[step]).wait()
+            wait_sent.append(pltpu.make_async_copy(buffer, buffer, red_send.at[step]).wait)
 
     reduce_send(0, peers_1, part, gather_1)
     second = (send_2, recv_2)
@@ -492,6 +505,8 @@
     reduce_wait(1, gather_2)
     for d in range(7):
         total = total + gather_2[d].astype(f32)
+    for wait in wait_sent:
+        wait()
     wgrad_ref[...] = total * (1.0 / math.sqrt(CZ * CY * X * n_a * n_b))
 
 

time: 31.6 us -> 31 us (0.981)
  Pallas kernels: 30.8 us -> 30.3 us
    pallas_call x1, Pallas kernels: 29.8 us -> 29.3 us  [fused(): pl.pallas_call(functools.partial(kernel, comm=comm), out_shape=[shape((CH...]
where the time goes in v7:
time: 31 us; the launch traced here: 30.9 us
  Pallas kernels  30.3 us (98%)
  between operations  0.64 us (2%)
    pallas_call x1, Pallas kernels, fused(): pl.pallas_call(functools.partial(kernel, comm=comm), out_shape=[shape((CH...  29.3 us
    pallas_call x1, Pallas kernels, fused(): pl.pallas_call(copy_kernel, out_shape=[shape((CH, slots_all), bf16), shap...  1.03 us

profile of v7, /device:TPU:1, one launch (start us, length us, event | category | flops | bytes accessed | tf_op | source)
XLA Modules:
  0.0 30.9 jit_solution(1119348338753177029)
XLA Ops:
  0.6 29.3 %shard_map.85 = (bf16[16,17920]{1,0:T(8,128)(2,1)S(1)}, bf16[16,17920]{1,0:T(8,128)(2,1)S(1)}, f32[16,128]{1,0:T(8,128)S(1)}) custom-call(bf16[16,14336]{1,0:T(8,128)(2,1)} %feats_hbm.1, bf16[16,17920]{1,0:T(8,128)(2,1)} %cot_hbm.1, s32[112,128]{1,0:T(8,128)} %bitcast.7, s32[1,2,1792]{2,1,0:T(2,128)} %slots_hbm.1, s32[1,2]{1,0:T(1,128)} %count_hbm.1, ...), custom_call_target="tpu_custom_call" | custom-call | tf_op jit(solution)/shard_map/pallas_call | solution.py:538
  29.9 1.0 %shard_map.86 = (bf16[16,17920]{1,0:T(8,128)(2,1)}, bf16[16,17920]{1,0:T(8,128)(2,1)}, f32[27,4,16]{2,1,0:T(4,128)}) custom-call(bf16[16,17920]{1,0:T(8,128)(2,1)S(1)} %get-tuple-element.9.out, bf16[16,17920]{1,0:T(8,128)(2,1)S(1)} %get-tuple-element.10.grad, f32[16,128]{1,0:T(8,128)S(1)} %get-tuple-element.11.total), custom_call_target="tpu_custom_call" | custom-call | tf_op jit(solution)/shard_map/pallas_call | solution.py:596

commit v8 on v7

--- a/solution.py
+++ b/solution.py
@@ -103,7 +103,7 @@
     around = [(da, db) for da in (-1, 0, 1) for db in (-1, 0, 1) if (da, db) != (0, 0)]
     if comm:
         barrier = pltpu.get_barrier_semaphore()
-        for place in [near(da, db) for da, db in around] + peers_1 + peers_2:
+        for place in peers_2 + peers_1 + [near(da, db) for da, db in around]:
             pl.semaphore_signal(barrier, inc=1, device_id=place, device_id_type=MESH)
 
     tap_row = lax.broadcasted_iota(jnp.int32, (144, 128), 0)
@@ -450,7 +450,7 @@
             into[:, pl.ds(pl.multiple_of(k * S, 128), S)] = select(found, codes[k])
             return carry
 
-        lax.fori_loop(0, ALL, body, 0, unroll=5)
+        lax.fori_loop(0, ALL, body, 0, unroll=10)
 
     read_back(act, out_buf)
 

time: 31 us -> 31.1 us (level)
  no operation moved by 1% of the time
where the time goes in v8:
time: 31.1 us; the launch traced here: 31 us
  Pallas kernels  30.3 us (97%)
  between operations  0.64 us (2%)
    pallas_call x1, Pallas kernels, fused(): pl.pallas_call(functools.partial(kernel, comm=comm), out_shape=[shape((CH...  29.3 us
    pallas_call x1, Pallas kernels, fused(): pl.pallas_call(copy_kernel, out_shape=[shape((CH, slots_all), bf16), shap...  1.03 us

profile of v8, /device:TPU:1, one launch (start us, length us, event | category | flops | bytes accessed | tf_op | source)
XLA Modules:
  0.0 31.0 jit_solution(2007092108909115621)
XLA Ops:
  0.6 29.3 %shard_map.85 = (bf16[16,17920]{1,0:T(8,128)(2,1)S(1)}, bf16[16,17920]{1,0:T(8,128)(2,1)S(1)}, f32[16,128]{1,0:T(8,128)S(1)}) custom-call(bf16[16,14336]{1,0:T(8,128)(2,1)} %feats_hbm.1, bf16[16,17920]{1,0:T(8,128)(2,1)} %cot_hbm.1, s32[112,128]{1,0:T(8,128)} %bitcast.7, s32[1,2,1792]{2,1,0:T(2,128)} %slots_hbm.1, s32[1,2]{1,0:T(1,128)} %count_hbm.1, ...), custom_call_target="tpu_custom_call" | custom-call | tf_op jit(solution)/shard_map/pallas_call | solution.py:538
  29.9 1.0 %shard_map.86 = (bf16[16,17920]{1,0:T(8,128)(2,1)}, bf16[16,17920]{1,0:T(8,128)(2,1)}, f32[27,4,16]{2,1,0:T(4,128)}) custom-call(bf16[16,17920]{1,0:T(8,128)(2,1)S(1)} %get-tuple-element.9.out, bf16[16,17920]{1,0:T(8,128)(2,1)S(1)} %get-tuple-element.10.grad, f32[16,128]{1,0:T(8,128)S(1)} %get-tuple-element.11.total), custom_call_target="tpu_custom_call" | custom-call | tf_op jit(solution)/shard_map/pallas_call | solution.py:596
